TPU v7x, 512 devices: a whole 4x4x16 slice. The times are simulated.
512 devices in a mesh: sta: 64 (over x_hi, z, core), win: 8 (over y, x_lo).
Axes of the slice: x: 4 (x_hi: 2, x_lo: 2; x = x_hi * 2 + x_lo), y: 4, z: 16, core: 2. Of those that a mesh axis runs over, the one named last changes fastest.
Arguments:
- phases: bfloat16 [64, 1024, 1024], P('win', 'sta'), may hold values from -3.140625 to 3.140625
- validity: int32 [64, 1024], P('win', 'sta'), may hold values from 0 to 1, as said below
- plan: int32 [4], replicated, may hold values from 0 to 63
Outputs:
- correlation: bfloat16 [4, 16, 1024, 256], P(None, 'win', 'sta')
Inputs may be any that keep to these rules, and one draw needn't show every extreme that they name: `plan`: each entry names a block of 16 consecutive stations. `validity`: 0 or 1; some stations have no usable window at all.
All inputs are finite; a program needn't handle non-finite values.
Results may differ from a plain program's by a relative error of at most 0.015.
Values may be sent and summed in bfloat16 or wider, within the bound.
No kernel may reach another device: no remote copies, remote signals or barrier semaphores. Data moves between devices by JAX's collectives and lax.ppermute only.
A program may use at most 64 MiB of HBM per device.

v0:
```python
import math

import jax
import jax.numpy as jnp
from jax import lax
from jax.sharding import PartitionSpec as P

LAGS = 256
SRC = 16
STEPS = 4


def spread(value, axis, source):
    kept = jnp.where(lax.axis_index(axis) == source, value, 0).astype(value.dtype)
    return lax.psum(kept, axis)


def idft_table(bins, lags):
    frequency = jnp.arange(bins, dtype=jnp.int32)[:, None]
    lag_offset = jnp.arange(lags, dtype=jnp.int32)[None, :] - lags // 2
    phase_turns = jnp.mod(frequency * lag_offset, 2 * bins).astype(jnp.float32)
    angles = phase_turns * (math.pi / bins)
    return jnp.concatenate([jnp.cos(angles), -jnp.sin(angles)], 0).astype(jnp.bfloat16)


def window_sum(first_src, first_recv, second_src, second_recv, sign):
    left_one = first_src[:, :, None, :].astype(jnp.float32)
    right_one = first_recv[:, None, :, :].astype(jnp.float32)
    left_two = second_src[:, :, None, :].astype(jnp.float32)
    right_two = second_recv[:, None, :, :].astype(jnp.float32)
    return jnp.sum(left_one * right_one + sign * (left_two * right_two), axis=0)


def cross_lags(source, receivers, lag_table):
    half_bins = source.shape[-1] // 2
    source_re, source_im = (source[..., :half_bins], source[..., half_bins:])
    recv_re, recv_im = (receivers[..., :half_bins], receivers[..., half_bins:])
    real_part = window_sum(source_re, recv_re, source_im, recv_im, 1.0)
    imag_part = window_sum(source_im, recv_re, source_re, recv_im, -1.0)
    stacked = jnp.concatenate([real_part, imag_part], -1).astype(jnp.bfloat16)
    flat = stacked.reshape(-1, 2 * half_bins)
    lagged = jnp.dot(flat, lag_table, preferred_element_type=jnp.float32)
    return lagged.reshape(source.shape[1], receivers.shape[1], lag_table.shape[1])


def step_term(source, spectra, lag_table):
    return cross_lags(source, spectra, lag_table)


def on_device(phases, validity, plan):
    windows_here, stations_here, bins = phases.shape
    source_share = SRC // lax.axis_size("win")
    lag_table = idft_table(bins, LAGS)
    station_flags = validity.astype(jnp.float32)
    values = phases.astype(jnp.float32)
    spectra = (
        jnp.concatenate([jnp.cos(values), jnp.sin(values)], -1) * station_flags[..., None]
    ).astype(jnp.bfloat16)
    flags_half = validity.astype(jnp.bfloat16)
    blocks_here = stations_here // SRC
    sources = []
    counts = []
    lag_parts = []
    for step_index in range(STEPS):
        block_id = plan[step_index]
        owner_index = block_id // blocks_here
        source, source_flags = (
            spread(spectra, "sta", owner_index),
            spread(flags_half, "sta", owner_index),
        )
        sources.append(source)
        counts.append(jnp.dot(source_flags.T, flags_half, preferred_element_type=jnp.float32))
        full_term = step_term(source, spectra, lag_table)
        summed_lags = lax.psum(full_term.astype(jnp.bfloat16), "win").astype(jnp.float32)
        lag_parts.append(
            lax.dynamic_slice_in_dim(
                summed_lags, lax.axis_index("win") * source_share, source_share, 0
            )
        )
    lag_sum = jnp.stack(lag_parts, 0)
    count_all = jnp.stack(counts, 0)
    summed = lax.psum(count_all, "win")
    pair_count = lax.dynamic_slice_in_dim(
        summed, lax.axis_index("win") * source_share, source_share, 1
    )
    factor = 1.0 / (math.sqrt(bins) * jnp.sqrt(jnp.maximum(pair_count, 1.0)))
    return (lag_sum * factor[..., None]).astype(jnp.bfloat16)


def solution(mesh):
    return jax.shard_map(
        on_device,
        mesh=mesh,
        in_specs=(P("win", "sta", None), P("win", "sta"), P()),
        out_specs=P(None, "win", "sta", None),
        check_vma=False,
    )
```

profile of v0, /device:TPU:1, one launch (start us, length us, event | category | flops | bytes accessed | tf_op | source)
XLA Modules:
  0.0 662.0 jit_solution(17428729588350331422)
XLA Ops:
  6.5 0.0 all-reduce.6.cloned.1.call-start
  6.5 1.5 fusion.25
  8.0 2.8 convert_cosine_fusion
  13.3 1.0 broadcast_select_fusion
  14.3 1.2 broadcast_select_fusion.1
  15.5 0.0 all-reduce.6.cloned.1.call-update
  15.6 0.0 all-reduce.8.cloned.1.call-start
  15.6 138.6 %all-reduce = (bf16[8,16]{1,0:T(8,128)(2,1)S(1)}, bf16[8,16]{1,0:T(8,128)(2,1)S(1)}, bf16[8,16]{1,0:T(8,128)(2,1)S(1)}, bf16[8,16]{1,0:T(8,128)(2,1)S(1)}) all-reduce(bf16[8,16]{1,0:T(8,128)(2,1)S(1)} %get-tuple-element.51, bf16[8,16]{1,0:T(8,128)(2,1)S(1)} %get-tuple-element.52, ...), channel_id=1, replica_groups=mesh['sta'=64,'win'=8] {'sta'}, use_global_device_ids=true, to_apply=%region_19.20 | all-reduce | flops 512 | bytes 2048 | tf_op jit(solution)/shard_map/psum | solution.py:15
  154.3 0.2 convolution_bitcast_fusion
  154.4 5.0 cosine_convert_fusion
  159.5 0.1 slice_convert_fusion.8
  159.6 388.8 %all-reduce.6.cloned.1.call-done = (bf16[8,16,2048]{2,1,0:T(8,128)(2,1)}, bf16[8,16,2048]{2,1,0:T(8,128)(2,1)}, bf16[8,16,2048]{2,1,0:T(8,128)(2,1)}, bf16[8,16,2048]{2,1,0:T(8,128)(2,1)}) async-done(((bf16[8,16,2048]{2,1,0:T(8,128)(2,1)}, bf16[8,16,2048]{2,1,0:T(8,128)(2,1)}, bf16[8,16,2048]{2,1,0:T(8,128)(2,1)}, bf16[8,16,2048]{2,1,0:T(8,128)(2,1)}), (bf16[8,16,2048]{2,1,0:T(8,128)(2,1)}, ...) | async-done | bytes 2097168 | tf_op jit(solution)/shard_map/psum | solution.py:15
  548.4 1.5 slice_convert_fusion
  549.9 0.0 copy-done.7
  549.9 0.2 slice_convert_fusion.4
  550.1 15.3 %add_reduce_fusion.7 = (bf16[16,16,1024]{2,1,0:T(8,128)(2,1)}, bf16[16,16,1024]{2,1,0:T(8,128)(2,1)}, bf16[16,16,1024]{2,1,0:T(8,128)(2,1)}, bf16[16,16,1024]{2,...) fusion(f32[8,16,1024]{2,1,0:T(8,128)S(1)} %get-tuple-element.44, ...), kind=kLoop, calls=%fused_computation.7 | loop fusion | flops 73400320 | bytes 9437184 | tf_op jit(solution)/shard_map/reduce_sum | solution.py:31
  565.4 2.7 convolution_convert_fusion.3
  568.2 1.1 convolution_convert_fusion.2
  569.3 0.1 copy-done.1
  569.4 1.1 convolution_convert_fusion.1
  570.4 1.1 convolution_convert_fusion
  571.5 0.0 all-reduce.8.cloned.1.call-update
  571.6 0.2 convolution_bitcast_fusion.1
  571.7 0.2 convolution_bitcast_fusion.2
  571.9 0.2 convolution_bitcast_fusion.3
  572.1 26.9 %psum.103 = f32[4,16,16]{2,1,0:T(8,128)S(1)} all-reduce(f32[4,16,16]{2,1,0:T(8,128)S(1)} %pad_maximum_fusion), channel_id=1, replica_groups=mesh['sta'=64,'win'=8] {'win'}, use_global_device_ids=true, to_apply=%region_20.21 | all-reduce | flops 1024 | bytes 8192 | tf_op jit(solution)/shard_map/psum | solution.py:82
  599.1 52.5 %all-reduce.8.cloned.1.call-done = (bf16[16,16,256]{2,1,0:T(8,128)(2,1)}, bf16[16,16,256]{2,1,0:T(8,128)(2,1)}, bf16[16,16,256]{2,1,0:T(8,128)(2,1)}, bf16[16,16,256]{2,1,0:T(8,128)(2,1)}) async-done(((bf16[16,16,256]{2,1,0:T(8,128)(2,1)}, bf16[16,16,256]{2,1,0:T(8,128)(2,1)}, bf16[16,16,256]{2,1,0:T(8,128)(2,1)}, bf16[16,16,256]{2,1,0:T(8,128)(2,1)}), (bf16[16,16,256]{2,1,0:T(8,128)(2,1)}, ...) | async-done | bytes 524304 | tf_op jit(solution)/shard_map/psum | solution.py:74
  651.5 0.7 convert_bitcast_fusion.1
  652.3 0.7 convert_bitcast_fusion.2
  653.0 0.7 convert_bitcast_fusion.3
  653.7 0.7 convert_bitcast_fusion
  654.4 0.7 fusion.19
  (22 shorter events, 0.1 us)
Async XLA Ops:
  6.5 541.8 %all-reduce.6.cloned.1.call-start = ((), (), s32[]{:S(2)}) async-start(), calls=%async_computation | async-start | bytes 4194304 | tf_op jit(solution)/shard_map/psum | solution.py:15
  8.0 2.8 copy-start.8
  15.6 636.0 %all-reduce.8.cloned.1.call-start = ((), (), s32[]{:S(2)}) async-start(), calls=%async_computation.1 | async-start | bytes 1048576 | tf_op jit(solution)/shard_map/psum | solution.py:74
  548.4 1.5 copy-start.6
  548.4 1.5 copy-start.7
  565.4 2.8 copy-start.2
  565.4 2.8 copy-start.3
  565.4 2.8 copy-start.4
  565.4 2.8 copy-start.5
  568.1 1.1 copy-start
  568.2 1.2 copy-start.1
Sparse Core Ops, SparseCore 0:
  15.7 532.6 all-reduce.5
  571.7 79.8 all-reduce.7
where the time goes:
time: 666 us; the launch traced here: 662 us
  waiting for transfers between devices  441 us (66%)
  blocking collectives  166 us (25%)
  other arithmetic  30.7 us (5%)
  between operations  16.1 us (2%)
  matrix products  6.75 us (1%)
    psum x1, waiting for transfers between devices, spread(): return lax.psum(kept, axis)  389 us
    psum x1, blocking collectives, spread(): return lax.psum(kept, axis)  139 us
    psum x1, waiting for transfers between devices, on_device(): lax.psum(full_term.astype(jnp.bfloat16), 'win').astype(jnp.float32)  52.5 us
    psum x1, blocking collectives, on_device(): summed = lax.psum(count_all, 'win')  26.9 us
    reduce_sum x1, other arithmetic, window_sum(): return jnp.sum(left_one * right_one + sign * (left_two * right_two), axis=0)  15.3 us
  transfers between devices with their start and end apart: 2, of which 2 were waited for; matrix products, arithmetic and copies ran while one was open for 1% of the time, Pallas kernels for 0%

commit v1 on v0

v1 whole, which is shorter than its diff:
```python
import math

import jax
import jax.numpy as jnp
from jax import lax
from jax.sharding import PartitionSpec as P

LAGS = 256
SRC = 16
STEPS = 4
N_Z = 16
N_WIN = 8
N_STA = 64
FLAG_LANES = 128

SAME_Z = [[32 * h + 2 * z + c for h in range(2) for c in range(2)] for z in range(N_Z)]
ALONG_Z = [[32 * h + 2 * z + c for z in range(N_Z)] for h in range(2) for c in range(2)]
QUADS = [
    [w * N_STA + 4 * i + j for w in range(N_WIN) for j in range(4)] for i in range(N_STA // 4)
]


def xor_pairs(size, mask):
    return [(i, i ^ mask) for i in range(size)]


def idft_table(bins, lags):
    frequency = jnp.arange(bins, dtype=jnp.int32)[:, None]
    lag_offset = jnp.arange(lags, dtype=jnp.int32)[None, :] - lags // 2
    phase_turns = jnp.mod(frequency * lag_offset, 2 * bins).astype(jnp.float32)
    angles = phase_turns * (math.pi / bins)
    return jnp.concatenate([jnp.cos(angles), -jnp.sin(angles)], 0).astype(jnp.bfloat16)


def spectra_of(rows, bins):
    values = rows[..., :bins].astype(jnp.float32)
    flags = rows[..., bins : bins + 1].astype(jnp.float32)
    return jnp.cos(values) * flags, jnp.sin(values) * flags, flags[..., 0]


def on_device(phases, validity, plan):
    windows_here, stations_here, bins = phases.shape
    width = bins + FLAG_LANES
    me = lax.axis_index("sta")
    quad_place = lax.rem(me, 4)
    core = lax.rem(me, 2)
    flags = jnp.broadcast_to(
        validity.astype(jnp.bfloat16)[..., None], (windows_here, stations_here, FLAG_LANES)
    )
    own = jnp.concatenate([phases, flags], -1)

    two = jnp.stack([own, lax.ppermute(own, "sta", xor_pairs(N_STA, 1))], 0)
    four = jnp.concatenate([two, lax.ppermute(two, "sta", xor_pairs(N_STA, 2))], 0)

    pieces = lax.all_to_all(
        own.reshape(N_Z, 8, width), "sta", 0, 0, tiled=True, axis_index_groups=ALONG_Z
    )
    owner_z = lax.rem(plan // 2, N_Z)
    owner_place = 2 * (plan // 32) + lax.rem(plan, 2)
    held = jnp.stack([lax.dynamic_index_in_dim(pieces, owner_z[k], 0, False) for k in range(STEPS)])
    by_core = held.reshape(2, 2, 8, width).transpose(1, 0, 2, 3)
    sent = jnp.broadcast_to(by_core[None], (2, 2, 2, 8, width)).reshape(4, 2, 8, width)
    came = lax.all_to_all(sent, "sta", 0, 0, tiled=True, axis_index_groups=SAME_Z)
    mine = jnp.stack(
        [
            lax.dynamic_slice(
                came, (owner_place[2 * half + core], half, 0, 0), (1, 1, 8, width)
            ).reshape(8, width)
            for half in range(2)
        ]
    )
    source = lax.all_to_all(
        jnp.tile(mine, (N_Z // 2, 1, 1)), "sta", 0, 0, tiled=True, axis_index_groups=ALONG_Z
    ).reshape(windows_here, SRC, width)

    src_re, src_im, src_flags = spectra_of(source, bins)
    receivers = four.transpose(1, 0, 2, 3)[:, quad_place ^ jnp.arange(4)].reshape(
        windows_here, 4 * stations_here, width
    )
    rec_re, rec_im, rec_flags = spectra_of(receivers, bins)

    def over_windows(one, two, three, four, sign):
        return jnp.sum(
            one[:, :, None] * two[:, None] + sign * (three[:, :, None] * four[:, None]), 0
        )

    real_part = over_windows(src_re, rec_re, src_im, rec_im, 1.0)
    imag_part = over_windows(src_im, rec_re, src_re, rec_im, -1.0)
    stacked = jnp.concatenate([real_part, imag_part], -1).astype(jnp.bfloat16)
    lagged = jnp.dot(
        stacked.reshape(-1, 2 * bins), idft_table(bins, LAGS), preferred_element_type=jnp.float32
    ).astype(jnp.bfloat16)
    counts = jnp.dot(
        src_flags.T.astype(jnp.bfloat16),
        rec_flags.astype(jnp.bfloat16),
        preferred_element_type=jnp.float32,
    ).astype(jnp.bfloat16)

    lag_pieces = lagged.reshape(N_WIN, 2, 4, stations_here, LAGS).transpose(0, 2, 1, 3, 4)
    lag_pieces = lag_pieces.reshape(N_WIN * 4, 2 * stations_here, LAGS)
    count_pieces = counts.reshape(N_WIN, 2, 4, stations_here).transpose(0, 2, 1, 3)
    count_pieces = count_pieces.reshape(N_WIN * 4, 2, stations_here)
    count_pieces = jnp.pad(count_pieces, ((0, 0), (0, 6), (0, LAGS - stations_here)))
    back = lax.all_to_all(
        jnp.concatenate([lag_pieces, count_pieces], 1),
        ("win", "sta"),
        0,
        0,
        tiled=True,
        axis_index_groups=QUADS,
    )
    total = jnp.sum(back.reshape(N_WIN, 4, 2 * stations_here + 8, LAGS).astype(jnp.float32), 0)
    lag_sum = total[:, : 2 * stations_here].reshape(STEPS, 2, stations_here, LAGS)
    pair_count = total[:, 2 * stations_here : 2 * stations_here + 2, :stations_here]
    factor = 1.0 / (math.sqrt(bins) * jnp.sqrt(jnp.maximum(pair_count, 1.0)))
    return (lag_sum * factor[..., None]).astype(jnp.bfloat16)


def solution(mesh):
    return jax.shard_map(
        on_device,
        mesh=mesh,
        in_specs=(P("win", "sta", None), P("win", "sta"), P()),
        out_specs=P(None, "win", "sta", None),
        check_vma=False,
    )
```

time: 666 us -> 122 us (0.18)
  waiting for transfers between devices: 441 us -> 7.48 us
  blocking collectives: 166 us -> 21.1 us
  starting transfers between devices: 0.04 us -> 37.8 us
    psum x2 -> x0, waiting for transfers between devices: 441 us -> none  [the longest x1 389 us: spread(): return lax.psum(kept, axis)]
    psum x2 -> x0, blocking collectives: 166 us -> none  [the longest x1 139 us: spread(): return lax.psum(kept, axis)]
    all_to_all x0 -> x3, starting transfers between devices: none -> 31.9 us  [the longest x1 15.7 us: on_device(): lax.all_to_all(own.reshape(N_Z, 8, width), 'sta', 0, 0, tiled=True, axis_...]
    all_to_all x0 -> x1, blocking collectives: none -> 21.1 us  [on_device(): lax.all_to_all(jnp.concatenate([lag_pieces, count_pieces], 1), ('win', 's...]
    mul x0 -> x4, other arithmetic: none -> 10.2 us  [spectra_of(): return (jnp.cos(values) * flags, jnp.sin(values) * flags, flags[..., 0])]
    all_to_all x0 -> x3, waiting for transfers between devices: none -> 7.47 us  [the longest x1 5.36 us: on_device(): lax.all_to_all(jnp.tile(mine, (N_Z // 2, 1, 1)), 'sta', 0, 0, tiled=True,...]
    reduce_sum x1 -> x2, other arithmetic: 15.3 us -> 17.3 us  [the longest x1 17.2 us: over_windows(): jnp.sum(one[:, :, None] * two[:, None] + sign * (three[:, :, None] * four...]
  transfers between devices with their start and end apart: 2 -> 5, of which waited for: 2 -> 2; matrix products, arithmetic and copies ran while one was open for 1% -> 14% of each run, Pallas kernels for 0% -> 0%
where the time goes in v1:
time: 122 us; the launch traced here: 121 us
  starting transfers between devices  37.8 us (31%)
  other arithmetic  36.6 us (30%)
  blocking collectives  21.1 us (17%)
  between operations  11.6 us (10%)
  waiting for transfers between devices  7.48 us (6%)
  local copies, waits for them, and re-layouts  3.45 us (3%)
  matrix products  3.03 us (2%)
    all_to_all x1, blocking collectives, on_device(): lax.all_to_all(jnp.concatenate([lag_pieces, count_pieces], 1), ('win', 's...  21.1 us
    reduce_sum x1, other arithmetic, over_windows(): jnp.sum(one[:, :, None] * two[:, None] + sign * (three[:, :, None] * four...  17.2 us
    all_to_all x1, starting transfers between devices, on_device(): lax.all_to_all(own.reshape(N_Z, 8, width), 'sta', 0, 0, tiled=True, axis_...  15.7 us
    mul x4, other arithmetic, spectra_of(): return (jnp.cos(values) * flags, jnp.sin(values) * flags, flags[..., 0])  10.2 us
    all_to_all x1, starting transfers between devices, on_device(): lax.all_to_all(sent, 'sta', 0, 0, tiled=True, axis_index_groups=SAME_Z)  8.87 us
    all_to_all x1, starting transfers between devices, on_device(): lax.all_to_all(jnp.tile(mine, (N_Z // 2, 1, 1)), 'sta', 0, 0, tiled=True,...  7.27 us
    all_to_all x1, waiting for transfers between devices, on_device(): lax.all_to_all(jnp.tile(mine, (N_Z // 2, 1, 1)), 'sta', 0, 0, tiled=True,...  5.36 us
    another operation x1, other arithmetic  5.06 us
  transfers between devices with their start and end apart: 5, of which 2 were waited for; matrix products, arithmetic and copies ran while one was open for 14% of the time, Pallas kernels for 0%

profile of v1, /device:TPU:1, one launch (start us, length us, event | category | flops | bytes accessed | tf_op | source)
XLA Modules:
  0.0 121.0 jit_solution(1751996100491059952)
XLA Ops:
  0.0 0.7 convert_element_type.39
  0.7 0.1 broadcast_in_dim.4
  0.8 1.7 %fusion.28 = (bf16[1,8,16,1152]{3,2,0,1:T(8,128)(2,1)S(1)}, bf16[8,16,1152]{2,1,0:T(8,128)(2,1)}) fusion(bf16[8,16,128]{2,1,0:T(8,128)(2,1)S(1)} %broadcast_in_dim.4, bf16[8,16,1024]{2,1,0:T(8,128)(2,1)} %param.3), kind=kLoop, calls=%fused_computation.70 | loop fusion | flops 589824 | bytes 884736 | tf_op jit(solution)/shard_map/stack | solution.py:52
  2.5 15.7 %all-to-all-start = ((bf16[16,8,1152]{2,1,0:T(8,128)(2,1)}), bf16[16,8,1152]{2,1,0:T(8,128)(2,1)S(1)}, u32[]{:S(2)}, u32[]{:S(2)}) async-start(bf16[16,8,1152]{2,1,0:T(8,128)(2,1)} %bitcast), calls=%async_computation | async-start | bytes 589824 | tf_op jit(solution)/shard_map/all_to_all | solution.py:55
  18.2 2.9 %collective-permute-start = (bf16[8,16,1152]{2,1,0:T(8,128)(2,1)}, bf16[8,16,1152]{2,1,0:T(8,128)(2,1)S(1)}, u32[]{:S(2)}, u32[]{:S(2)}) collective-permute-start(bf16[8,16,1152]{2,1,0:T(8,128)(2,1)} %get-tuple-element.12), channel_id=1, source_target_pairs={{0,8},{8,0},{16,24},{24,16},{32,40},{40,32},{48,56},{56,48},{64,72... | collective-permute-start | bytes 884744 | tf_op jit(solution)/shard_map/ppermute | solution.py:52
  21.1 0.7 multiply_add_fusion
  21.8 0.7 fusion.29
  33.9 0.7 broadcast_in_dim.5
  34.6 8.9 %all-to-all-start.1 = ((bf16[4,2,8,1152]{3,2,1,0:T(8,128)(2,1)}), bf16[4,2,8,1152]{3,2,1,0:T(8,128)(2,1)S(1)}, u32[]{:S(2)}, u32[]{:S(2)}) async-start(bf16[4,2,8,1152]{3,2,1,0:T(8,128)(2,1)} %bitcast.7), calls=%async_computation.1 | async-start | bytes 294912 | tf_op jit(solution)/shard_map/all_to_all | solution.py:63
  43.5 0.1 pad_maximum_fusion
  43.5 3.0 %collective-permute-start.1 = (bf16[2,8,16,1152]{3,2,0,1:T(8,128)(2,1)S(1)}, bf16[2,8,16,1152]{3,2,0,1:T(8,128)(2,1)S(1)}, u32[]{:S(2)}, u32[]{:S(2)}) collective-permute-start(bf16[2,8,16,1152]{3,2,0,1:T(8,128)(2,1)S(1)} %pad_maximum_fusion), channel_id=1, source_target_pairs={{0,16},{8,24},{16,0},{24,8},{32,48},{40,56},{48,32},{56,40},{64,80... | collective-permute-start | bytes 1769480 | tf_op jit(solution)/shard_map/ppermute | solution.py:53
  46.6 2.1 %all-to-all-done.1 = bf16[4,2,8,1152]{3,2,1,0:T(8,128)(2,1)S(1)} async-done(((bf16[4,2,8,1152]{3,2,1,0:T(8,128)(2,1)}), bf16[4,2,8,1152]{3,2,1,0:T(8,128)(2,1)S(1)}, u32[]{:S(2)}, u32[]{:S(2)}) %all-to-all-start.1) | async-done | bytes 147488 | tf_op jit(solution)/shard_map/all_to_all | solution.py:63
  48.7 0.7 tile.4
  49.5 7.3 %all-to-all-start.2 = ((bf16[16,8,1152]{2,1,0:T(8,128)(2,1)}), bf16[16,8,1152]{2,1,0:T(8,128)(2,1)S(1)}, u32[]{:S(2)}, u32[]{:S(2)}) async-start(bf16[16,8,1152]{2,1,0:T(8,128)(2,1)} %bitcast.12), calls=%async_computation.2 | async-start | bytes 589824 | tf_op jit(solution)/shard_map/all_to_all | solution.py:72
  56.7 5.1 %cosine_convert_fusion = (bf16[1024,256]{1,0:T(8,128)(2,1)}, bf16[1024,256]{1,0:T(8,128)(2,1)}) fusion(s32[256]{0:T(256)S(1)} %iota_add_fusion), kind=kLoop, calls=%fused_computation.27 | loop fusion | flops 4456448 | bytes 1049600 | tf_op jit(solution)/shard_map/convert.3
  61.8 0.1 maximum_bitcast_fusion
  61.9 0.7 gather_fusion
  62.7 0.1 copy.21
  62.8 0.1 slice_reduce_fusion
  62.9 8.3 %fusion.4 = (f32[8,64,1024]{2,1,0:T(8,128)S(1)}, f32[8,64,1024]{2,1,0:T(8,128)}) fusion(f32[8,64]{1,0:T(8,128)S(1)} %mul.139, bf16[8,64,1152]{2,1,0:T(8,128)(2,1)S(1)} %bitcast.45), kind=kLoop, calls=%fused_computation.9 | loop fusion | flops 1572864 | bytes 5244928 | tf_op jit(solution)/shard_map/mul | solution.py:38
  71.2 5.4 %all-to-all-done.2 = bf16[16,8,1152]{2,1,0:T(8,128)(2,1)S(1)} async-done(((bf16[16,8,1152]{2,1,0:T(8,128)(2,1)}), bf16[16,8,1152]{2,1,0:T(8,128)(2,1)S(1)}, u32[]{:S(2)}, u32[]{:S(2)}) %all-to-all-start.2) | async-done | bytes 294944 | tf_op jit(solution)/shard_map/all_to_all | solution.py:72
  76.6 0.1 slice_reduce_fusion.1
  76.7 0.2 convolution_convert_fusion
  76.9 1.9 %fusion.20 = (f32[8,16,1024]{2,1,0:T(8,128)S(1)}, f32[8,16,1024]{2,1,0:T(8,128)S(1)}) fusion(f32[8,16]{1,0:T(8,128)S(1)} %mul.134, bf16[8,16,1152]{2,1,0:T(8,128)(2,1)S(1)} %bitcast.53), kind=kLoop, calls=%fused_computation.35 | loop fusion | flops 393216 | bytes 1311232 | tf_op jit(solution)/shard_map/mul | solution.py:38
  78.8 17.2 %add_reduce_fusion.1 = (bf16[16,64,1024]{2,1,0:T(8,128)(2,1)S(1)}, bf16[16,64,1024]{2,1,0:T(8,128)(2,1)}) fusion(f32[8,64,1024]{2,1,0:T(8,128)} %get-tuple-element.8, f32[8,16,1024]{2,1,0:T(8,128)S(1)} %get-tuple-element.10, f32[8,64,1024]{2,1,0:T(8,128)S(1)} %get-tuple-element.7, f32[8,16,1024]{2,1,0:T(8,128)S(1)} %get-tuple-element.9), kind=kLoop, calls=%fused_computation.2 | loop fusion | flops 73400320 | bytes 9437184 | tf_op jit(solution)/shard_map/reduce_sum | solution.py:83
  96.0 2.8 %fusion.7 = bf16[1024,256]{1,0:T(8,128)(2,1)S(1)} fusion(bf16[1024,1024]{1,0:T(8,128)(2,1)} %bitcast.49, bf16[1024,1024]{1,0:T(8,128)(2,1)S(1)} %bitcast.48, bf16[1024,256]{1,0:T(8,128)(2,1)S(1)} %copy-done.1, bf16[1024,256]{1,0:T(8,128)(2,1)S(1)} %copy-done), kind=kOutput, calls=%fused_computation.17 | convolution fusion | flops 1084489728 | bytes 5767168 | tf_op jit(solution)/shard_map/dot_general | solution.py:90
  98.8 0.1 copy.22
  98.9 0.1 reshape.77
  99.0 0.1 fusion.19
  99.1 21.1 %all_to_all.20 = bf16[32,40,256]{2,1,0:T(8,128)(2,1)S(1)} all-to-all(bf16[32,40,256]{2,1,0:T(8,128)(2,1)S(1)} %fusion.19), channel_id=1, replica_groups={{0,8,16,24,1,9,17,25,2,10,18,26,3,11,19,27,4,12,20,28,5,13,21,29,6,14,2..., dimensions={0} | all-to-all | bytes 1310720 | tf_op jit(solution)/shard_map/all_to_all | solution.py:104
  120.2 0.1 convert_reduce_fusion
  120.3 0.7 multiply_convert_fusion
  (21 shorter events, 0.2 us)
Async XLA Ops:
  2.5 31.4 %all-to-all-start = ((bf16[16,8,1152]{2,1,0:T(8,128)(2,1)}), bf16[16,8,1152]{2,1,0:T(8,128)(2,1)S(1)}, u32[]{:S(2)}, u32[]{:S(2)}) async-start(bf16[16,8,1152]{2,1,0:T(8,128)(2,1)} %bitcast), calls=%async_computation | async-start | bytes 589824 | tf_op jit(solution)/shard_map/all_to_all | solution.py:55
  18.2 25.2 %collective-permute-start = (bf16[8,16,1152]{2,1,0:T(8,128)(2,1)}, bf16[8,16,1152]{2,1,0:T(8,128)(2,1)S(1)}, u32[]{:S(2)}, u32[]{:S(2)}) collective-permute-start(bf16[8,16,1152]{2,1,0:T(8,128)(2,1)} %get-tuple-element.12), channel_id=1, source_target_pairs={{0,8},{8,0},{16,24},{24,16},{32,40},{40,32},{48,56},{56,48},{64,72... | collective-permute-start | bytes 884744 | tf_op jit(solution)/shard_map/ppermute | solution.py:52
  34.6 14.1 %all-to-all-start.1 = ((bf16[4,2,8,1152]{3,2,1,0:T(8,128)(2,1)}), bf16[4,2,8,1152]{3,2,1,0:T(8,128)(2,1)S(1)}, u32[]{:S(2)}, u32[]{:S(2)}) async-start(bf16[4,2,8,1152]{3,2,1,0:T(8,128)(2,1)} %bitcast.7), calls=%async_computation.1 | async-start | bytes 294912 | tf_op jit(solution)/shard_map/all_to_all | solution.py:63
  43.5 18.3 %collective-permute-start.1 = (bf16[2,8,16,1152]{3,2,0,1:T(8,128)(2,1)S(1)}, bf16[2,8,16,1152]{3,2,0,1:T(8,128)(2,1)S(1)}, u32[]{:S(2)}, u32[]{:S(2)}) collective-permute-start(bf16[2,8,16,1152]{3,2,0,1:T(8,128)(2,1)S(1)} %pad_maximum_fusion), channel_id=1, source_target_pairs={{0,16},{8,24},{16,0},{24,8},{32,48},{40,56},{48,32},{56,40},{64,80... | collective-permute-start | bytes 1769480 | tf_op jit(solution)/shard_map/ppermute | solution.py:53
  49.5 27.1 %all-to-all-start.2 = ((bf16[16,8,1152]{2,1,0:T(8,128)(2,1)}), bf16[16,8,1152]{2,1,0:T(8,128)(2,1)S(1)}, u32[]{:S(2)}, u32[]{:S(2)}) async-start(bf16[16,8,1152]{2,1,0:T(8,128)(2,1)} %bitcast.12), calls=%async_computation.2 | async-start | bytes 589824 | tf_op jit(solution)/shard_map/all_to_all | solution.py:72
  78.8 17.2 %copy-start = (bf16[1024,256]{1,0:T(8,128)(2,1)S(1)}, bf16[1024,256]{1,0:T(8,128)(2,1)}, u32[]{:S(2)}) copy-start(bf16[1024,256]{1,0:T(8,128)(2,1)} %get-tuple-element.19) | copy-start | bytes 1572868
  78.8 17.2 %copy-start.1 = (bf16[1024,256]{1,0:T(8,128)(2,1)S(1)}, bf16[1024,256]{1,0:T(8,128)(2,1)}, u32[]{:S(2)}) copy-start(bf16[1024,256]{1,0:T(8,128)(2,1)} %get-tuple-element.20) | copy-start | bytes 1572868

commit v2 on v1

v2 whole, which is shorter than its diff:
```python
import math

import jax
import jax.numpy as jnp
from jax import lax
from jax.experimental import pallas as pl
from jax.experimental.pallas import tpu as pltpu
from jax.sharding import PartitionSpec as P

BINS = 1024
LAGS = 256
SRC = 16
STEPS = 4
WIN_DEV = 8
N_Z = 16
N_WIN = 8
N_STA = 64
LANES = 128
CHUNKS = BINS // LANES
WIDTH = BINS + LANES
PIECE_ROWS = 72

QUAD = [[32 * h + 2 * z + c for h in range(2) for c in range(2)] for z in range(N_Z)]
ALONG_Z = [[32 * h + 2 * z + c for z in range(N_Z)] for h in range(2) for c in range(2)]
ALL_QUADS = [[w * N_STA + i for w in range(N_WIN) for i in quad] for quad in QUAD]
MASKS = (0, 2, 1, 3)

SINE = (
    0.7071067690849304,
    -0.029462749138474464,
    0.0003682656097225845,
    -2.1877108338230755e-06,
    7.1552790359419305e-09,
)
COSINE = (
    1.4142135381698608,
    -0.17677636444568634,
    0.003682575421407819,
    -3.061264942516573e-05,
    1.2790856374067516e-07,
)


def xor_pairs(mask):
    return [(i, i ^ mask) for i in range(N_STA)]


def idft_table(bins, lags):
    frequency = jnp.arange(bins, dtype=jnp.int32)[:, None]
    lag_offset = jnp.arange(lags, dtype=jnp.int32)[None, :] - lags // 2
    phase_turns = jnp.mod(frequency * lag_offset, 2 * bins).astype(jnp.float32)
    angles = phase_turns * (math.pi / bins)
    return jnp.concatenate([jnp.cos(angles), -jnp.sin(angles)], 0).astype(jnp.bfloat16)


def cos_sin(x):
    square = x * x
    sine, cosine = SINE[-1], COSINE[-1]
    for a, b in zip(SINE[-2::-1], COSINE[-2::-1]):
        sine = sine * square + a
        cosine = cosine * square + b
    sine = sine * x
    return 1.0 - sine * sine, sine * cosine


def receivers_kernel(one_ref, two_ref, re_ref, im_ref, flag_ref):
    lanes = lax.broadcasted_iota(jnp.int32, (SRC, LANES), 1)
    for group, ref in enumerate((one_ref, two_ref)):
        for place in range(2):
            rows = slice(32 * group + SRC * place, 32 * group + SRC * place + SRC)

            def window(w, marks):
                flag = ref[place, w, :, BINS:].astype(jnp.float32)
                for c in range(CHUNKS):
                    cols = slice(LANES * c, LANES * c + LANES)
                    re, im = cos_sin(ref[place, w, :, cols].astype(jnp.float32))
                    re_ref[w, rows, cols] = (re * flag).astype(jnp.bfloat16)
                    im_ref[w, rows, cols] = (im * flag).astype(jnp.bfloat16)
                return marks + jnp.where(lanes == w, flag, 0.0)

            marks = lax.fori_loop(0, WIN_DEV, window, jnp.zeros((SRC, LANES), jnp.float32))
            flag_ref[rows, :] = marks.astype(jnp.bfloat16)


def receivers(one, two):
    spectrum = jax.ShapeDtypeStruct((WIN_DEV, 4 * SRC, BINS), jnp.bfloat16)
    return pl.pallas_call(
        receivers_kernel,
        out_shape=[spectrum, spectrum, jax.ShapeDtypeStruct((4 * SRC, LANES), jnp.bfloat16)],
        compiler_params=pltpu.CompilerParams(vmem_limit_bytes=32 << 20),
        cost_estimate=pl.CostEstimate(
            flops=25 * 4 * SRC * WIN_DEV * BINS, bytes_accessed=4 << 20, transcendentals=0
        ),
        name="receivers",
    )(one, two)


def correlate_kernel(
    place_ref, src_ref, re_ref, im_ref, flag_ref, table_ref, out_ref, src_re, src_im, stacked
):
    lanes = lax.broadcasted_iota(jnp.int32, (SRC, LANES), 1)
    place = place_ref[0]
    marks = jnp.zeros((SRC, LANES), jnp.float32)
    for w in range(WIN_DEV):
        flag = src_ref[SRC * w : SRC * w + SRC, BINS:].astype(jnp.float32)
        marks = marks + jnp.where(lanes == w, flag, 0.0)
    marks = marks.astype(jnp.bfloat16)

    def prepare(c, carry):
        cols = pl.ds(pl.multiple_of(c * LANES, LANES), LANES)
        for w in range(WIN_DEV):
            rows = slice(SRC * w, SRC * w + SRC)
            flag = src_ref[rows, BINS:].astype(jnp.float32)
            re, im = cos_sin(src_ref[rows, cols].astype(jnp.float32))
            re, im = re * flag, im * flag
            for s in range(SRC):
                wide = (SRC, LANES)
                src_re[c, SRC * w + s] = jnp.broadcast_to(re[s : s + 1], wide).astype(jnp.bfloat16)
                src_im[c, SRC * w + s] = jnp.broadcast_to(im[s : s + 1], wide).astype(jnp.bfloat16)
        return carry

    lax.fori_loop(0, CHUNKS, prepare, 0)
    for half in range(2):

        def chunk(c, carry):
            cols = pl.ds(pl.multiple_of(c * LANES, LANES), LANES)
            later = pl.ds(pl.multiple_of(BINS + c * LANES, LANES), LANES)
            blocks = [slice(32 * half + SRC * h, 32 * half + SRC * h + SRC) for h in range(2)]
            rec_re = [[re_ref[w, rows, cols] for rows in blocks] for w in range(WIN_DEV)]
            rec_im = [[im_ref[w, rows, cols] for rows in blocks] for w in range(WIN_DEV)]
            for s in range(SRC):
                real, imag = [[], []], [[], []]
                for w in range(WIN_DEV):
                    a, b = src_re[c, SRC * w + s], src_im[c, SRC * w + s]
                    for h in range(2):
                        real[h].append(a * rec_re[w][h] + b * rec_im[w][h])
                        imag[h].append(b * rec_re[w][h] - a * rec_im[w][h])
                for h in range(2):
                    for terms, place_of in ((real[h], cols), (imag[h], later)):
                        while len(terms) > 1:
                            terms = [terms[i] + terms[i + 1] for i in range(0, len(terms), 2)]
                        stacked[2 * half + h, SRC * s : SRC * s + SRC, place_of] = terms[0]
            return carry

        lax.fori_loop(0, CHUNKS, chunk, 0)
    for d in range(4):
        lags = jnp.dot(stacked[d], table_ref[...], preferred_element_type=jnp.float32)
        lags = lags.astype(jnp.bfloat16)
        count = lax.dot_general(
            marks,
            flag_ref[SRC * d : SRC * d + SRC, :],
            (((1,), (1,)), ((), ())),
            preferred_element_type=jnp.float32,
        )
        count = jnp.concatenate([count, jnp.zeros((SRC, LANES - SRC), jnp.float32)], 1)
        count = count.astype(jnp.bfloat16)
        to = place ^ MASKS[d]
        for w in range(N_WIN):
            out_ref[w, to, 0:32, :] = lags[32 * w : 32 * w + 32, :LANES]
            out_ref[w, to, 32:64, :] = lags[32 * w : 32 * w + 32, LANES:]
            first = 8 * (w // 4)
            out_ref[w, to, 64:PIECE_ROWS, :] = count[first : first + 8]


def correlate(place, source, rec_re, rec_im, rec_flags, table):
    vmem = pl.BlockSpec(memory_space=pltpu.VMEM)
    return pl.pallas_call(
        correlate_kernel,
        out_shape=jax.ShapeDtypeStruct((N_WIN, 4, PIECE_ROWS, LANES), jnp.bfloat16),
        in_specs=[pl.BlockSpec(memory_space=pltpu.SMEM)] + [vmem] * 5,
        out_specs=vmem,
        scratch_shapes=[pltpu.VMEM((CHUNKS, WIN_DEV * SRC, SRC, LANES), jnp.bfloat16)] * 2
        + [pltpu.VMEM((4, SRC * SRC, 2 * BINS), jnp.bfloat16)],
        compiler_params=pltpu.CompilerParams(vmem_limit_bytes=40 << 20),
        cost_estimate=pl.CostEstimate(flops=1 << 30, bytes_accessed=4 << 20, transcendentals=0),
        name="correlate",
    )(place, source, rec_re, rec_im, rec_flags, table)


def on_device(phases, validity, plan):
    me = lax.axis_index("sta")
    place = 2 * (me // 32) + lax.rem(me, 2)
    flags = jnp.broadcast_to(
        validity.astype(jnp.bfloat16)[..., None], (WIN_DEV, SRC, LANES)
    )
    own = jnp.concatenate([phases, flags], -1)

    one = jnp.stack([own, lax.ppermute(own, "sta", xor_pairs(32))], 0)
    two = lax.ppermute(one, "sta", xor_pairs(1))
    rec_re, rec_im, rec_flags = receivers(one, two)

    pieces = lax.all_to_all(
        own.reshape(N_Z, 8, WIDTH), "sta", 0, 0, tiled=True, axis_index_groups=ALONG_Z
    )
    owner_z = lax.rem(plan // 2, N_Z)
    owner_place = 2 * (plan // 32) + lax.rem(plan, 2)
    held = jnp.stack(
        [lax.dynamic_index_in_dim(pieces, owner_z[k], 0, False) for k in range(STEPS)]
    )
    came = lax.all_to_all(held, "sta", 0, 0, tiled=True, axis_index_groups=QUAD)
    mine = lax.dynamic_slice_in_dim(came, owner_place[place], 1, 0)
    source = lax.all_to_all(
        jnp.broadcast_to(mine, (N_Z, 8, WIDTH)),
        "sta",
        0,
        0,
        tiled=True,
        axis_index_groups=ALONG_Z,
    ).reshape(WIN_DEV * SRC, WIDTH)

    sent = correlate(place[None], source, rec_re, rec_im, rec_flags, idft_table(BINS, LAGS))
    back = lax.all_to_all(
        sent.reshape(N_WIN * 4, PIECE_ROWS, LANES),
        ("win", "sta"),
        0,
        0,
        tiled=True,
        axis_index_groups=ALL_QUADS,
    )
    total = jnp.sum(back.reshape(N_WIN, 4, PIECE_ROWS, LANES).astype(jnp.float32), 0)
    lag_sum = total[:, :64].reshape(STEPS, 2, 2, SRC, LANES).transpose(0, 2, 3, 1, 4)
    lag_sum = lag_sum.reshape(STEPS, 2, SRC, LAGS)
    first = 64 + 2 * lax.rem(lax.axis_index("win"), 4)
    pair_count = lax.dynamic_slice(total, (0, first, 0), (STEPS, 2, SRC))
    factor = 1.0 / (math.sqrt(BINS) * jnp.sqrt(jnp.maximum(pair_count, 1.0)))
    return (lag_sum * factor[..., None]).astype(jnp.bfloat16)


def solution(mesh):
    return jax.shard_map(
        on_device,
        mesh=mesh,
        in_specs=(P("win", "sta", None), P("win", "sta"), P()),
        out_specs=P(None, "win", "sta", None),
        check_vma=False,
    )
```

time: 122 us -> 110 us (0.902)
  other arithmetic: 36.6 us -> 8.46 us
  blocking collectives: 21.1 us -> 0 us
  Pallas kernels: 0 us -> 15 us
  waiting for transfers between devices: 7.48 us -> 22.4 us
  starting transfers between devices: 37.8 us -> 51 us
  matrix products: 3.03 us -> 0 us
  between operations: 11.6 us -> 9.61 us
    all_to_all x1 -> x0, blocking collectives: 21.1 us -> none  [on_device(): lax.all_to_all(jnp.concatenate([lag_pieces, count_pieces], 1), ('win', 's...]
    reduce_sum x2 -> x1, other arithmetic: 17.3 us -> 0.08 us  [on_device(): jnp.sum(back.reshape(N_WIN, 4, PIECE_ROWS, LANES).astype(jnp.float32), 0)]
    pallas_call x0 -> x2, Pallas kernels: none -> 15 us  [the longest x1 12.9 us: correlate(): pl.pallas_call(correlate_kernel, out_shape=jax.ShapeDtypeStruct((N_WIN, 4...]
    all_to_all x3 -> x4, waiting for transfers between devices: 7.47 us -> 22.4 us  [the longest x1 12.2 us: on_device(): lax.all_to_all(sent.reshape(N_WIN * 4, PIECE_ROWS, LANES), ('win', 'sta')...]
    all_to_all x3 -> x4, starting transfers between devices: 31.9 us -> 43.4 us  [the longest x1 15.7 us: on_device(): lax.all_to_all(own.reshape(N_Z, 8, WIDTH), 'sta', 0, 0, tiled=True, axis_...]
    mul x4 -> x0, other arithmetic: 10.2 us -> none  [spectra_of(): return (jnp.cos(values) * flags, jnp.sin(values) * flags, flags[..., 0])]
    dot_general x2 -> x0, matrix products: 3.03 us -> none  [the longest x1 2.85 us: on_device(): jnp.dot(stacked.reshape(-1, 2 * bins), idft_table(bins, LAGS), preferred_...]
    ppermute x2, starting transfers between devices: 5.9 us -> 7.61 us  [the longest x1 4.79 us: on_device(): one = jnp.stack([own, lax.ppermute(own, 'sta', xor_pairs(32))], 0)]
  transfers between devices with their start and end apart: 5 -> 6, of which waited for: 2 -> 3; matrix products, arithmetic and copies ran while one was open for 14% -> 6% of each run, Pallas kernels for 0% -> 2%
where the time goes in v2:
time: 110 us; the launch traced here: 109 us
  starting transfers between devices  51 us (46%)
  waiting for transfers between devices  22.4 us (20%)
  Pallas kernels  15 us (14%)
  between operations  9.61 us (9%)
  other arithmetic  8.46 us (8%)
  local copies, waits for them, and re-layouts  2.37 us (2%)
    all_to_all x1, starting transfers between devices, on_device(): lax.all_to_all(own.reshape(N_Z, 8, WIDTH), 'sta', 0, 0, tiled=True, axis_...  15.7 us
    pallas_call x1, Pallas kernels, correlate(): pl.pallas_call(correlate_kernel, out_shape=jax.ShapeDtypeStruct((N_WIN, 4...  12.9 us
    all_to_all x1, waiting for transfers between devices, on_device(): lax.all_to_all(sent.reshape(N_WIN * 4, PIECE_ROWS, LANES), ('win', 'sta')...  12.2 us
    all_to_all x1, starting transfers between devices, on_device(): lax.all_to_all(sent.reshape(N_WIN * 4, PIECE_ROWS, LANES), ('win', 'sta')...  10.9 us
    all_to_all x1, starting transfers between devices, on_device(): came = lax.all_to_all(held, 'sta', 0, 0, tiled=True, axis_index_groups=QUAD)  10.8 us
    all_to_all x1, starting transfers between devices, on_device(): lax.all_to_all(jnp.broadcast_to(mine, (N_Z, 8, WIDTH)), 'sta', 0, 0, tile...  6 us
    all_to_all x1, waiting for transfers between devices, on_device(): lax.all_to_all(own.reshape(N_Z, 8, WIDTH), 'sta', 0, 0, tiled=True, axis_...  5.69 us
    ppermute x1, starting transfers between devices, on_device(): one = jnp.stack([own, lax.ppermute(own, 'sta', xor_pairs(32))], 0)  4.79 us
  transfers between devices with their start and end apart: 6, of which 3 were waited for; matrix products, arithmetic and copies ran while one was open for 6% of the time, Pallas kernels for 2%

profile of v2, /device:TPU:1, one launch (start us, length us, event | category | flops | bytes accessed | tf_op | source)
XLA Modules:
  0.0 108.9 jit_solution(1513992683174904225)
XLA Ops:
  0.0 0.0 copy-start
  0.0 0.7 convert_element_type.18
  0.7 0.1 broadcast_in_dim.9
  0.8 1.7 %fusion.7 = (bf16[1,8,16,1152]{3,2,1,0:T(8,128)(2,1)S(1)}, bf16[8,16,1152]{2,1,0:T(8,128)(2,1)}) fusion(bf16[8,16,128]{2,1,0:T(8,128)(2,1)S(1)} %broadcast_in_dim.9, bf16[8,16,1024]{2,1,0:T(8,128)(2,1)} %param.3), kind=kLoop, calls=%fused_computation.37 | loop fusion | flops 589824 | bytes 884736 | tf_op jit(solution)/shard_map/stack | solution.py:188
  2.5 15.7 %all-to-all-start = ((bf16[16,8,1152]{2,1,0:T(8,128)(2,1)}), bf16[16,8,1152]{2,1,0:T(8,128)(2,1)S(1)}, u32[]{:S(2)}, u32[]{:S(2)}) async-start(bf16[16,8,1152]{2,1,0:T(8,128)(2,1)} %bitcast.1), calls=%async_computation | async-start | bytes 589824 | tf_op jit(solution)/shard_map/all_to_all | solution.py:192
  18.2 0.0 copy-done
  18.3 0.7 fusion.8
  26.3 5.7 %all-to-all-done = bf16[16,8,1152]{2,1,0:T(8,128)(2,1)S(1)} async-done(((bf16[16,8,1152]{2,1,0:T(8,128)(2,1)}), bf16[16,8,1152]{2,1,0:T(8,128)(2,1)S(1)}, u32[]{:S(2)}, u32[]{:S(2)}) %all-to-all-start) | async-done | bytes 294944 | tf_op jit(solution)/shard_map/all_to_all | solution.py:192
  32.0 0.7 pad_maximum_fusion.3
  32.7 10.8 %all-to-all-start.1 = ((bf16[4,8,1152]{2,1,0:T(8,128)(2,1)}), bf16[4,8,1152]{2,1,0:T(8,128)(2,1)S(1)}, u32[]{:S(2)}, u32[]{:S(2)}) async-start(bf16[4,8,1152]{2,1,0:T(8,128)(2,1)} %pad_maximum_fusion.3), calls=%async_computation.1 | async-start | bytes 147456 | tf_op jit(solution)/shard_map/all_to_all | solution.py:200
  43.4 4.8 %collective-permute-start = (bf16[8,16,1152]{2,1,0:T(8,128)(2,1)}, bf16[8,16,1152]{2,1,0:T(8,128)(2,1)S(1)}, u32[]{:S(2)}, u32[]{:S(2)}) collective-permute-start(bf16[8,16,1152]{2,1,0:T(8,128)(2,1)} %get-tuple-element.12), channel_id=1, source_target_pairs={{0,256},{8,264},{16,272},{24,280},{32,288},{40,296},{48,304},{56,3... | collective-permute-start | bytes 884744 | tf_op jit(solution)/shard_map/ppermute | solution.py:188
  48.2 0.7 dynamic_slice.26
  50.9 0.0 all-to-all-done.1
  51.0 0.7 broadcast_in_dim.22
  51.7 6.0 %all-to-all-start.2 = ((bf16[16,8,1152]{2,1,0:T(8,128)(2,1)}), bf16[16,8,1152]{2,1,0:T(8,128)(2,1)S(1)}, u32[]{:S(2)}, u32[]{:S(2)}) async-start(bf16[16,8,1152]{2,1,0:T(8,128)(2,1)} %broadcast_in_dim.22), calls=%async_computation.2 | async-start | bytes 589824 | tf_op jit(solution)/shard_map/all_to_all | solution.py:202
  57.7 0.0 collective-permute-done
  57.7 0.1 pad_maximum_fusion.1.one_ref
  57.8 2.8 %collective-permute-start.1 = (bf16[2,8,16,1152]{3,2,1,0:T(8,128)(2,1)S(1)}, bf16[2,8,16,1152]{3,2,1,0:T(8,128)(2,1)S(1)}, u32[]{:S(2)}, u32[]{:S(2)}) collective-permute-start(bf16[2,8,16,1152]{3,2,1,0:T(8,128)(2,1)S(1)} %pad_maximum_fusion.1.one_ref), channel_id=1, source_target_pairs={{0,8},{8,0},{16,24},{24,16},{32,40},{40,32},{48,56},{56,48},{64,72... | collective-permute-start | bytes 1769480 | tf_op jit(solution)/shard_map/ppermute | solution.py:189
  60.6 4.4 %cosine_convert_fusion = (bf16[1024,256]{1,0:T(8,128)(2,1)S(1)}, bf16[1024,256]{1,0:T(8,128)(2,1)S(1)}) fusion(s32[256]{0:T(256)S(1)} %iota_add_fusion), kind=kLoop, calls=%fused_computation.9 | loop fusion | flops 4456448 | bytes 1049600 | tf_op jit(solution)/shard_map/convert.1
  65.1 0.1 pad_maximum_fusion.table_ref
  65.2 0.0 collective-permute-done.1.two_ref
  65.2 2.1 %receivers.1 = (bf16[8,64,1024]{2,1,0:T(8,128)(2,1)S(1)}, bf16[8,64,1024]{2,1,0:T(8,128)(2,1)S(1)}, bf16[64,128]{1,0:T(8,128)(2,1)S(1)}) custom-call(bf16[2,8,16,1152]{3,2,1,0:T(8,128)(2,1)S(1)} %pad_maximum_fusion.1.one_ref, bf16[2,8,16,1152]{3,2,1,0:T(8,128)(2,1)S(1)} %collective-permute-done.1.two_ref), custom_call_target="tpu_custom_call" | custom-call | flops 13107200 | bytes 4194304 | tf_op jit(solution)/shard_map/receivers/pallas_call | solution.py:87
  67.2 4.6 %all-to-all-done.2 = bf16[16,8,1152]{2,1,0:T(8,128)(2,1)S(1)} async-done(((bf16[16,8,1152]{2,1,0:T(8,128)(2,1)}), bf16[16,8,1152]{2,1,0:T(8,128)(2,1)S(1)}, u32[]{:S(2)}, u32[]{:S(2)}) %all-to-all-start.2) | async-done | bytes 294944 | tf_op jit(solution)/shard_map/all_to_all | solution.py:202
  71.8 12.9 %correlate.1 = bf16[8,4,72,128]{3,2,1,0:T(8,128)(2,1)} custom-call(s32[1]{0:T(128)} %bitcast.place_ref, bf16[128,1152]{1,0:T(8,128)(2,1)S(1)} %bitcast.20, bf16[8,64,1024]{2,1,0:T(8,128)(2,1)S(1)} %get-tuple-element.8.re_ref, bf16[8,64,1024]{2,1,0:T(8,128)(2,1)S(1)} %get-tuple-element.9.im_ref, bf16[64,128]{1,0:T(8,128)(2,1)S(1)} %get-tuple-element.10.flag_ref, ...), custom_call_target="tpu_custom_call" | custom-call | flops 1073741824 | bytes 4194304 | tf_op jit(solution)/shard_map/correlate/pallas_call | solution.py:167
  84.8 10.9 %all-to-all-start.3 = ((bf16[32,72,128]{2,1,0:T(8,128)(2,1)}), bf16[32,72,128]{2,1,0:T(8,128)(2,1)S(1)}, u32[]{:S(2)}, u32[]{:S(2)}) async-start(bf16[32,72,128]{2,1,0:T(8,128)(2,1)} %bitcast.11), calls=%async_computation.3 | async-start | bytes 1179648 | tf_op jit(solution)/shard_map/all_to_all | solution.py:212
  95.6 12.2 %all-to-all-done.3 = bf16[32,72,128]{2,1,0:T(8,128)(2,1)S(1)} async-done(((bf16[32,72,128]{2,1,0:T(8,128)(2,1)}), bf16[32,72,128]{2,1,0:T(8,128)(2,1)S(1)}, u32[]{:S(2)}, u32[]{:S(2)}) %all-to-all-start.3) | async-done | bytes 589856 | tf_op jit(solution)/shard_map/all_to_all | solution.py:212
  107.8 0.1 convert_reduce_fusion
  107.9 0.1 copy.6
  108.0 0.1 reshape.29
  108.2 0.7 multiply_convert_fusion
  (6 shorter events, 0.1 us)
Async XLA Ops:
  0.0 18.2 %copy-start = (s32[4]{0:T(128)S(1)}, s32[4]{0:T(128)}, u32[]{:S(2)}) copy-start(s32[4]{0:T(128)} %param.5) | copy-start | bytes 52
  2.5 29.5 %all-to-all-start = ((bf16[16,8,1152]{2,1,0:T(8,128)(2,1)}), bf16[16,8,1152]{2,1,0:T(8,128)(2,1)S(1)}, u32[]{:S(2)}, u32[]{:S(2)}) async-start(bf16[16,8,1152]{2,1,0:T(8,128)(2,1)} %bitcast.1), calls=%async_computation | async-start | bytes 589824 | tf_op jit(solution)/shard_map/all_to_all | solution.py:192
  32.7 18.3 %all-to-all-start.1 = ((bf16[4,8,1152]{2,1,0:T(8,128)(2,1)}), bf16[4,8,1152]{2,1,0:T(8,128)(2,1)S(1)}, u32[]{:S(2)}, u32[]{:S(2)}) async-start(bf16[4,8,1152]{2,1,0:T(8,128)(2,1)} %pad_maximum_fusion.3), calls=%async_computation.1 | async-start | bytes 147456 | tf_op jit(solution)/shard_map/all_to_all | solution.py:200
  43.4 14.3 %collective-permute-start = (bf16[8,16,1152]{2,1,0:T(8,128)(2,1)}, bf16[8,16,1152]{2,1,0:T(8,128)(2,1)S(1)}, u32[]{:S(2)}, u32[]{:S(2)}) collective-permute-start(bf16[8,16,1152]{2,1,0:T(8,128)(2,1)} %get-tuple-element.12), channel_id=1, source_target_pairs={{0,256},{8,264},{16,272},{24,280},{32,288},{40,296},{48,304},{56,3... | collective-permute-start | bytes 884744 | tf_op jit(solution)/shard_map/ppermute | solution.py:188
  51.7 20.1 %all-to-all-start.2 = ((bf16[16,8,1152]{2,1,0:T(8,128)(2,1)}), bf16[16,8,1152]{2,1,0:T(8,128)(2,1)S(1)}, u32[]{:S(2)}, u32[]{:S(2)}) async-start(bf16[16,8,1152]{2,1,0:T(8,128)(2,1)} %broadcast_in_dim.22), calls=%async_computation.2 | async-start | bytes 589824 | tf_op jit(solution)/shard_map/all_to_all | solution.py:202
  57.8 7.4 %collective-permute-start.1 = (bf16[2,8,16,1152]{3,2,1,0:T(8,128)(2,1)S(1)}, bf16[2,8,16,1152]{3,2,1,0:T(8,128)(2,1)S(1)}, u32[]{:S(2)}, u32[]{:S(2)}) collective-permute-start(bf16[2,8,16,1152]{3,2,1,0:T(8,128)(2,1)S(1)} %pad_maximum_fusion.1.one_ref), channel_id=1, source_target_pairs={{0,8},{8,0},{16,24},{24,16},{32,40},{40,32},{48,56},{56,48},{64,72... | collective-permute-start | bytes 1769480 | tf_op jit(solution)/shard_map/ppermute | solution.py:189
  84.8 23.0 %all-to-all-start.3 = ((bf16[32,72,128]{2,1,0:T(8,128)(2,1)}), bf16[32,72,128]{2,1,0:T(8,128)(2,1)S(1)}, u32[]{:S(2)}, u32[]{:S(2)}) async-start(bf16[32,72,128]{2,1,0:T(8,128)(2,1)} %bitcast.11), calls=%async_computation.3 | async-start | bytes 1179648 | tf_op jit(solution)/shard_map/all_to_all | solution.py:212

commit v3 on v2

--- a/solution.py
+++ b/solution.py
@@ -22,7 +22,10 @@
 
 QUAD = [[32 * h + 2 * z + c for h in range(2) for c in range(2)] for z in range(N_Z)]
 ALONG_Z = [[32 * h + 2 * z + c for z in range(N_Z)] for h in range(2) for c in range(2)]
-ALL_QUADS = [[w * N_STA + i for w in range(N_WIN) for i in quad] for quad in QUAD]
+ALL_QUADS = [
+    [w * N_STA + 32 * h + 2 * z + c for w in range(N_WIN) for h in range(2) for c in range(2)]
+    for z in range(N_Z)
+]
 MASKS = (0, 2, 1, 3)
 
 SINE = (
@@ -63,6 +66,27 @@
     return 1.0 - sine * sine, sine * cosine
 
 
+def pack_kernel(phases_ref, validity_ref, out_ref):
+    flags = validity_ref[...].astype(jnp.float32)
+    here = lax.broadcasted_iota(jnp.int32, (SRC, SRC), 0)
+    here = here == lax.broadcasted_iota(jnp.int32, (SRC, SRC), 1)
+    for w in range(WIN_DEV):
+        rows = slice(SRC * w, SRC * w + SRC)
+        out_ref[rows, :BINS] = phases_ref[w]
+        row = jnp.broadcast_to(flags[w : w + 1], (SRC, SRC))
+        column = jnp.sum(jnp.where(here, row, 0.0), 1, keepdims=True)
+        out_ref[rows, BINS:] = jnp.broadcast_to(column, (SRC, LANES)).astype(jnp.bfloat16)
+
+
+def pack(phases, validity):
+    return pl.pallas_call(
+        pack_kernel,
+        out_shape=jax.ShapeDtypeStruct((WIN_DEV * SRC, WIDTH), jnp.bfloat16),
+        cost_estimate=pl.CostEstimate(flops=0, bytes_accessed=600 << 10, transcendentals=0),
+        name="pack",
+    )(phases, validity)
+
+
 def receivers_kernel(one_ref, two_ref, re_ref, im_ref, flag_ref):
     lanes = lax.broadcasted_iota(jnp.int32, (SRC, LANES), 1)
     for group, ref in enumerate((one_ref, two_ref)):
@@ -96,7 +120,7 @@
 
 
 def correlate_kernel(
-    place_ref, src_ref, re_ref, im_ref, flag_ref, table_ref, out_ref, src_re, src_im, stacked
+    place_ref, src_ref, re_ref, im_ref, flag_ref, table_ref, out_ref, src_sum, src_re, src_im, stacked
 ):
     lanes = lax.broadcasted_iota(jnp.int32, (SRC, LANES), 1)
     place = place_ref[0]
@@ -108,38 +132,40 @@
 
     def prepare(c, carry):
         cols = pl.ds(pl.multiple_of(c * LANES, LANES), LANES)
-        for w in range(WIN_DEV):
-            rows = slice(SRC * w, SRC * w + SRC)
-            flag = src_ref[rows, BINS:].astype(jnp.float32)
-            re, im = cos_sin(src_ref[rows, cols].astype(jnp.float32))
-            re, im = re * flag, im * flag
-            for s in range(SRC):
-                wide = (SRC, LANES)
-                src_re[c, SRC * w + s] = jnp.broadcast_to(re[s : s + 1], wide).astype(jnp.bfloat16)
-                src_im[c, SRC * w + s] = jnp.broadcast_to(im[s : s + 1], wide).astype(jnp.bfloat16)
+        flag = src_ref[:, BINS:].astype(jnp.float32)
+        re, im = cos_sin(src_ref[:, cols].astype(jnp.float32))
+        re = (re * flag).astype(jnp.bfloat16).astype(jnp.float32)
+        im = (im * flag).astype(jnp.bfloat16).astype(jnp.float32)
+        src_re[c] = re
+        src_im[c] = im
+        src_sum[c] = re + im
         return carry
 
     lax.fori_loop(0, CHUNKS, prepare, 0)
-    for half in range(2):
+    for d in range(4):
 
         def chunk(c, carry):
             cols = pl.ds(pl.multiple_of(c * LANES, LANES), LANES)
             later = pl.ds(pl.multiple_of(BINS + c * LANES, LANES), LANES)
-            blocks = [slice(32 * half + SRC * h, 32 * half + SRC * h + SRC) for h in range(2)]
-            rec_re = [[re_ref[w, rows, cols] for rows in blocks] for w in range(WIN_DEV)]
-            rec_im = [[im_ref[w, rows, cols] for rows in blocks] for w in range(WIN_DEV)]
+            first, plus, minus = [], [], []
+            for w in range(WIN_DEV):
+                re = re_ref[w, SRC * d : SRC * d + SRC, cols].astype(jnp.float32)
+                im = im_ref[w, SRC * d : SRC * d + SRC, cols].astype(jnp.float32)
+                first.append(re)
+                plus.append(re + im)
+                minus.append(im - re)
             for s in range(SRC):
-                real, imag = [[], []], [[], []]
+                p = q = t = None
                 for w in range(WIN_DEV):
-                    a, b = src_re[c, SRC * w + s], src_im[c, SRC * w + s]
-                    for h in range(2):
-                        real[h].append(a * rec_re[w][h] + b * rec_im[w][h])
-                        imag[h].append(b * rec_re[w][h] - a * rec_im[w][h])
-                for h in range(2):
-                    for terms, place_of in ((real[h], cols), (imag[h], later)):
-                        while len(terms) > 1:
-                            terms = [terms[i] + terms[i + 1] for i in range(0, len(terms), 2)]
-                        stacked[2 * half + h, SRC * s : SRC * s + SRC, place_of] = terms[0]
+                    row = pl.ds(SRC * w + s, 1)
+                    wide = (SRC, LANES)
+                    both = jnp.broadcast_to(src_sum[c, row, :], wide) * first[w]
+                    real = jnp.broadcast_to(src_re[c, row, :], wide) * plus[w]
+                    imag = jnp.broadcast_to(src_im[c, row, :], wide) * minus[w]
+                    p, q, t = (both, real, imag) if w == 0 else (p + both, q + real, t + imag)
+                rows = slice(SRC * s, SRC * s + SRC)
+                stacked[d, rows, cols] = (p + t).astype(jnp.bfloat16)
+                stacked[d, rows, later] = (p - q).astype(jnp.bfloat16)
             return carry
 
         lax.fori_loop(0, CHUNKS, chunk, 0)
@@ -158,8 +184,8 @@
         for w in range(N_WIN):
             out_ref[w, to, 0:32, :] = lags[32 * w : 32 * w + 32, :LANES]
             out_ref[w, to, 32:64, :] = lags[32 * w : 32 * w + 32, LANES:]
-            first = 8 * (w // 4)
-            out_ref[w, to, 64:PIECE_ROWS, :] = count[first : first + 8]
+            up = 8 * (w // 4)
+            out_ref[w, to, 64:PIECE_ROWS, :] = count[up : up + 8]
 
 
 def correlate(place, source, rec_re, rec_im, rec_flags, table):
@@ -169,7 +195,7 @@
         out_shape=jax.ShapeDtypeStruct((N_WIN, 4, PIECE_ROWS, LANES), jnp.bfloat16),
         in_specs=[pl.BlockSpec(memory_space=pltpu.SMEM)] + [vmem] * 5,
         out_specs=vmem,
-        scratch_shapes=[pltpu.VMEM((CHUNKS, WIN_DEV * SRC, SRC, LANES), jnp.bfloat16)] * 2
+        scratch_shapes=[pltpu.VMEM((CHUNKS, WIN_DEV * SRC, LANES), jnp.float32)] * 3
         + [pltpu.VMEM((4, SRC * SRC, 2 * BINS), jnp.bfloat16)],
         compiler_params=pltpu.CompilerParams(vmem_limit_bytes=40 << 20),
         cost_estimate=pl.CostEstimate(flops=1 << 30, bytes_accessed=4 << 20, transcendentals=0),
@@ -180,25 +206,25 @@
 def on_device(phases, validity, plan):
     me = lax.axis_index("sta")
     place = 2 * (me // 32) + lax.rem(me, 2)
-    flags = jnp.broadcast_to(
-        validity.astype(jnp.bfloat16)[..., None], (WIN_DEV, SRC, LANES)
-    )
-    own = jnp.concatenate([phases, flags], -1)
-
-    one = jnp.stack([own, lax.ppermute(own, "sta", xor_pairs(32))], 0)
+    rows = pack(phases, validity)
+    own = rows.reshape(WIN_DEV, SRC, WIDTH)
+
+    across = lax.ppermute(own, "sta", xor_pairs(32))
+    pieces = lax.all_to_all(
+        rows.reshape(N_Z, 8, WIDTH), "sta", 0, 0, tiled=True, axis_index_groups=ALONG_Z
+    )
+    pieces, across = lax.optimization_barrier((pieces, across))
+    one = jnp.stack([own, across], 0)
     two = lax.ppermute(one, "sta", xor_pairs(1))
     rec_re, rec_im, rec_flags = receivers(one, two)
 
-    pieces = lax.all_to_all(
-        own.reshape(N_Z, 8, WIDTH), "sta", 0, 0, tiled=True, axis_index_groups=ALONG_Z
-    )
     owner_z = lax.rem(plan // 2, N_Z)
-    owner_place = 2 * (plan // 32) + lax.rem(plan, 2)
     held = jnp.stack(
         [lax.dynamic_index_in_dim(pieces, owner_z[k], 0, False) for k in range(STEPS)]
     )
     came = lax.all_to_all(held, "sta", 0, 0, tiled=True, axis_index_groups=QUAD)
-    mine = lax.dynamic_slice_in_dim(came, owner_place[place], 1, 0)
+    owner = plan[place]
+    mine = lax.dynamic_slice_in_dim(came, 2 * (owner // 32) + lax.rem(owner, 2), 1, 0)
     source = lax.all_to_all(
         jnp.broadcast_to(mine, (N_Z, 8, WIDTH)),
         "sta",

time: 110 us -> 105 us (0.955)
  waiting for transfers between devices: 22.4 us -> 18.1 us
  other arithmetic: 8.46 us -> 6.06 us
  starting transfers between devices: 51 us -> 53.2 us
    all_to_all x1, waiting for transfers between devices: 5.69 us -> 0.77 us  [on_device(): lax.all_to_all(rows.reshape(N_Z, 8, WIDTH), 'sta', 0, 0, tiled=True, axis...]
    pallas_call x1, Pallas kernels: 12.9 us -> 10.5 us  [correlate(): pl.pallas_call(correlate_kernel, out_shape=jax.ShapeDtypeStruct((N_WIN, 4...]
    all_to_all x1, starting transfers between devices: 10.9 us -> 12.8 us  [on_device(): lax.all_to_all(sent.reshape(N_WIN * 4, PIECE_ROWS, LANES), ('win', 'sta')...]
    pallas_call x0 -> x1, Pallas kernels: none -> 1.77 us  [pack(): pl.pallas_call(pack_kernel, out_shape=jax.ShapeDtypeStruct((WIN_DEV * SRC...]
    another operation x3 -> x2, other arithmetic: 6.2 us -> 4.5 us
    all_to_all x1, waiting for transfers between devices: 0.01 us -> 1.42 us  [on_device(): came = lax.all_to_all(held, 'sta', 0, 0, tiled=True, axis_index_groups=QUAD)]
  transfers between devices with their start and end apart: 6 -> 6, of which waited for: 3 -> 4; matrix products, arithmetic and copies ran while one was open for 6% -> 6% of each run, Pallas kernels for 2% -> 2%
where the time goes in v3:
time: 105 us; the launch traced here: 104 us
  starting transfers between devices  53.2 us (51%)
  waiting for transfers between devices  18.1 us (17%)
  Pallas kernels  14.3 us (14%)
  between operations  10.5 us (10%)
  other arithmetic  6.06 us (6%)
  local copies, waits for them, and re-layouts  2.28 us (2%)
    all_to_all x1, starting transfers between devices, on_device(): lax.all_to_all(rows.reshape(N_Z, 8, WIDTH), 'sta', 0, 0, tiled=True, axis...  15.9 us
    all_to_all x1, starting transfers between devices, on_device(): lax.all_to_all(sent.reshape(N_WIN * 4, PIECE_ROWS, LANES), ('win', 'sta')...  12.8 us
    all_to_all x1, waiting for transfers between devices, on_device(): lax.all_to_all(sent.reshape(N_WIN * 4, PIECE_ROWS, LANES), ('win', 'sta')...  12.2 us
    all_to_all x1, starting transfers between devices, on_device(): came = lax.all_to_all(held, 'sta', 0, 0, tiled=True, axis_index_groups=QUAD)  10.8 us
    pallas_call x1, Pallas kernels, correlate(): pl.pallas_call(correlate_kernel, out_shape=jax.ShapeDtypeStruct((N_WIN, 4...  10.5 us
    all_to_all x1, starting transfers between devices, on_device(): lax.all_to_all(jnp.broadcast_to(mine, (N_Z, 8, WIDTH)), 'sta', 0, 0, tile...  6 us
    ppermute x1, starting transfers between devices, on_device(): across = lax.ppermute(own, 'sta', xor_pairs(32))  4.65 us
    another operation x1, other arithmetic  4.43 us
  transfers between devices with their start and end apart: 6, of which 4 were waited for; matrix products, arithmetic and copies ran while one was open for 6% of the time, Pallas kernels for 2%

profile of v3, /device:TPU:1, one launch (start us, length us, event | category | flops | bytes accessed | tf_op | source)
XLA Modules:
  0.0 104.5 jit_solution(4212553470074731623)
XLA Ops:
  0.0 0.0 copy-start.1
  0.0 1.8 %pack.1 = bf16[128,1152]{1,0:T(8,128)(2,1)} custom-call(bf16[8,16,1024]{2,1,0:T(8,128)(2,1)} %phases_ref.1, s32[8,16]{1,0:T(8,128)} %validity_ref.1), custom_call_target="tpu_custom_call" | custom-call | bytes 614400 | tf_op jit(solution)/shard_map/pack/pallas_call | solution.py:82
  1.8 0.0 copy-start
  1.8 15.9 %all-to-all-start = ((bf16[16,8,1152]{2,1,0:T(8,128)(2,1)}), bf16[16,8,1152]{2,1,0:T(8,128)(2,1)S(1)}, u32[]{:S(2)}, u32[]{:S(2)}) async-start(bf16[16,8,1152]{2,1,0:T(8,128)(2,1)} %bitcast.21), calls=%async_computation | async-start | bytes 589824 | tf_op jit(solution)/shard_map/all_to_all | solution.py:213
  17.7 4.7 %collective-permute-start = (bf16[8,16,1152]{2,1,0:T(8,128)(2,1)}, bf16[8,16,1152]{2,1,0:T(8,128)(2,1)S(1)}, u32[]{:S(2)}, u32[]{:S(2)}) collective-permute-start(bf16[8,16,1152]{2,1,0:T(8,128)(2,1)} %bitcast.22), channel_id=1, source_target_pairs={{0,256},{8,264},{16,272},{24,280},{32,288},{40,296},{48,304},{56,3... | collective-permute-start | bytes 884744 | tf_op jit(solution)/shard_map/ppermute | solution.py:212
  22.3 0.0 copy-done.1
  22.4 0.7 fusion.7
  30.6 0.0 collective-permute-done
  30.7 0.8 all-to-all-done
  31.4 0.7 pad_maximum_fusion.2
  32.1 10.8 %all-to-all-start.1 = ((bf16[4,8,1152]{2,1,0:T(8,128)(2,1)}), bf16[4,8,1152]{2,1,0:T(8,128)(2,1)S(1)}, u32[]{:S(2)}, u32[]{:S(2)}) async-start(bf16[4,8,1152]{2,1,0:T(8,128)(2,1)} %pad_maximum_fusion.2), calls=%async_computation.1 | async-start | bytes 147456 | tf_op jit(solution)/shard_map/all_to_all | solution.py:225
  42.9 0.6 dynamic_slice.26
  46.2 1.4 %all-to-all-done.1 = bf16[4,8,1152]{2,1,0:T(8,128)(2,1)S(1)} async-done(((bf16[4,8,1152]{2,1,0:T(8,128)(2,1)}), bf16[4,8,1152]{2,1,0:T(8,128)(2,1)S(1)}, u32[]{:S(2)}, u32[]{:S(2)}) %all-to-all-start.1) | async-done | bytes 73760 | tf_op jit(solution)/shard_map/all_to_all | solution.py:225
  47.6 0.7 broadcast_in_dim.15
  48.4 6.0 %all-to-all-start.2 = ((bf16[16,8,1152]{2,1,0:T(8,128)(2,1)}), bf16[16,8,1152]{2,1,0:T(8,128)(2,1)S(1)}, u32[]{:S(2)}, u32[]{:S(2)}) async-start(bf16[16,8,1152]{2,1,0:T(8,128)(2,1)} %broadcast_in_dim.15), calls=%async_computation.2 | async-start | bytes 589824 | tf_op jit(solution)/shard_map/all_to_all | solution.py:228
  54.4 0.0 copy-done
  54.4 0.1 pad_maximum_fusion.1.one_ref
  54.5 3.1 %collective-permute-start.1 = (bf16[2,8,16,1152]{3,2,1,0:T(8,128)(2,1)S(1)}, bf16[2,8,16,1152]{3,2,1,0:T(8,128)(2,1)S(1)}, u32[]{:S(2)}, u32[]{:S(2)}) collective-permute-start(bf16[2,8,16,1152]{3,2,1,0:T(8,128)(2,1)S(1)} %pad_maximum_fusion.1.one_ref), channel_id=1, source_target_pairs={{0,8},{8,0},{16,24},{24,16},{32,40},{40,32},{48,56},{56,48},{64,72... | collective-permute-start | bytes 1769480 | tf_op jit(solution)/shard_map/ppermute | solution.py:218
  57.5 4.4 %cosine_convert_fusion = (bf16[1024,256]{1,0:T(8,128)(2,1)S(1)}, bf16[1024,256]{1,0:T(8,128)(2,1)S(1)}) fusion(s32[256]{0:T(256)S(1)} %iota_add_fusion), kind=kLoop, calls=%fused_computation.9 | loop fusion | flops 4456448 | bytes 1049600 | tf_op jit(solution)/shard_map/convert.1
  62.0 0.1 pad_maximum_fusion.table_ref
  62.1 0.0 collective-permute-done.1.two_ref
  62.1 2.1 %receivers.1 = (bf16[8,64,1024]{2,1,0:T(8,128)(2,1)S(1)}, bf16[8,64,1024]{2,1,0:T(8,128)(2,1)S(1)}, bf16[64,128]{1,0:T(8,128)(2,1)S(1)}) custom-call(bf16[2,8,16,1152]{3,2,1,0:T(8,128)(2,1)S(1)} %pad_maximum_fusion.1.one_ref, bf16[2,8,16,1152]{3,2,1,0:T(8,128)(2,1)S(1)} %collective-permute-done.1.two_ref), custom_call_target="tpu_custom_call" | custom-call | flops 13107200 | bytes 4194304 | tf_op jit(solution)/shard_map/receivers/pallas_call | solution.py:111
  64.1 3.8 %all-to-all-done.2 = bf16[16,8,1152]{2,1,0:T(8,128)(2,1)S(1)} async-done(((bf16[16,8,1152]{2,1,0:T(8,128)(2,1)}), bf16[16,8,1152]{2,1,0:T(8,128)(2,1)S(1)}, u32[]{:S(2)}, u32[]{:S(2)}) %all-to-all-start.2) | async-done | bytes 294944 | tf_op jit(solution)/shard_map/all_to_all | solution.py:228
  67.9 10.5 %correlate.1 = bf16[8,4,72,128]{3,2,1,0:T(8,128)(2,1)} custom-call(s32[1]{0:T(128)} %bitcast.place_ref, bf16[128,1152]{1,0:T(8,128)(2,1)S(1)} %bitcast.20, bf16[8,64,1024]{2,1,0:T(8,128)(2,1)S(1)} %get-tuple-element.12.re_ref, bf16[8,64,1024]{2,1,0:T(8,128)(2,1)S(1)} %get-tuple-element.13.im_ref, bf16[64,128]{1,0:T(8,128)(2,1)S(1)} %get-tuple-element.14.flag_ref, ...), custom_call_target="tpu_custom_call" | custom-call | flops 1073741824 | bytes 4194304 | tf_op jit(solution)/shard_map/correlate/pallas_call | solution.py:193
  78.4 12.8 %all-to-all-start.3 = ((bf16[32,72,128]{2,1,0:T(8,128)(2,1)}), bf16[32,72,128]{2,1,0:T(8,128)(2,1)S(1)}, u32[]{:S(2)}, u32[]{:S(2)}) async-start(bf16[32,72,128]{2,1,0:T(8,128)(2,1)} %bitcast.12), calls=%async_computation.3 | async-start | bytes 1179648 | tf_op jit(solution)/shard_map/all_to_all | solution.py:238
  91.2 12.2 %all-to-all-done.3 = bf16[32,72,128]{2,1,0:T(8,128)(2,1)S(1)} async-done(((bf16[32,72,128]{2,1,0:T(8,128)(2,1)}), bf16[32,72,128]{2,1,0:T(8,128)(2,1)S(1)}, u32[]{:S(2)}, u32[]{:S(2)}) %all-to-all-start.3) | async-done | bytes 589856 | tf_op jit(solution)/shard_map/all_to_all | solution.py:238
  103.4 0.1 convert_reduce_fusion
  103.5 0.1 copy.6
  103.6 0.1 reshape.32
  103.8 0.7 multiply_convert_fusion
  (6 shorter events, 0.1 us)
Async XLA Ops:
  0.0 22.3 %copy-start.1 = (s32[4]{0:T(128)S(1)}, s32[4]{0:T(128)}, u32[]{:S(2)}) copy-start(s32[4]{0:T(128)} %param.5) | copy-start | bytes 52
  1.8 52.6 %copy-start = (bf16[128,1152]{1,0:T(8,128)(2,1)S(1)}, bf16[128,1152]{1,0:T(8,128)(2,1)}, u32[]{:S(2)}) copy-start(bf16[128,1152]{1,0:T(8,128)(2,1)} %pack.1) | copy-start | bytes 884740
  1.8 29.6 %all-to-all-start = ((bf16[16,8,1152]{2,1,0:T(8,128)(2,1)}), bf16[16,8,1152]{2,1,0:T(8,128)(2,1)S(1)}, u32[]{:S(2)}, u32[]{:S(2)}) async-start(bf16[16,8,1152]{2,1,0:T(8,128)(2,1)} %bitcast.21), calls=%async_computation | async-start | bytes 589824 | tf_op jit(solution)/shard_map/all_to_all | solution.py:213
  17.7 13.0 %collective-permute-start = (bf16[8,16,1152]{2,1,0:T(8,128)(2,1)}, bf16[8,16,1152]{2,1,0:T(8,128)(2,1)S(1)}, u32[]{:S(2)}, u32[]{:S(2)}) collective-permute-start(bf16[8,16,1152]{2,1,0:T(8,128)(2,1)} %bitcast.22), channel_id=1, source_target_pairs={{0,256},{8,264},{16,272},{24,280},{32,288},{40,296},{48,304},{56,3... | collective-permute-start | bytes 884744 | tf_op jit(solution)/shard_map/ppermute | solution.py:212
  32.1 15.6 %all-to-all-start.1 = ((bf16[4,8,1152]{2,1,0:T(8,128)(2,1)}), bf16[4,8,1152]{2,1,0:T(8,128)(2,1)S(1)}, u32[]{:S(2)}, u32[]{:S(2)}) async-start(bf16[4,8,1152]{2,1,0:T(8,128)(2,1)} %pad_maximum_fusion.2), calls=%async_computation.1 | async-start | bytes 147456 | tf_op jit(solution)/shard_map/all_to_all | solution.py:225
  48.4 19.5 %all-to-all-start.2 = ((bf16[16,8,1152]{2,1,0:T(8,128)(2,1)}), bf16[16,8,1152]{2,1,0:T(8,128)(2,1)S(1)}, u32[]{:S(2)}, u32[]{:S(2)}) async-start(bf16[16,8,1152]{2,1,0:T(8,128)(2,1)} %broadcast_in_dim.15), calls=%async_computation.2 | async-start | bytes 589824 | tf_op jit(solution)/shard_map/all_to_all | solution.py:228
  54.5 7.6 %collective-permute-start.1 = (bf16[2,8,16,1152]{3,2,1,0:T(8,128)(2,1)S(1)}, bf16[2,8,16,1152]{3,2,1,0:T(8,128)(2,1)S(1)}, u32[]{:S(2)}, u32[]{:S(2)}) collective-permute-start(bf16[2,8,16,1152]{3,2,1,0:T(8,128)(2,1)S(1)} %pad_maximum_fusion.1.one_ref), channel_id=1, source_target_pairs={{0,8},{8,0},{16,24},{24,16},{32,40},{40,32},{48,56},{56,48},{64,72... | collective-permute-start | bytes 1769480 | tf_op jit(solution)/shard_map/ppermute | solution.py:218
  78.4 25.0 %all-to-all-start.3 = ((bf16[32,72,128]{2,1,0:T(8,128)(2,1)}), bf16[32,72,128]{2,1,0:T(8,128)(2,1)S(1)}, u32[]{:S(2)}, u32[]{:S(2)}) async-start(bf16[32,72,128]{2,1,0:T(8,128)(2,1)} %bitcast.12), calls=%async_computation.3 | async-start | bytes 1179648 | tf_op jit(solution)/shard_map/all_to_all | solution.py:238

commit v4 on v2

v4 whole, which is shorter than its diff:
```python
import math

import jax
import jax.numpy as jnp
from jax import lax
from jax.experimental import pallas as pl
from jax.experimental.pallas import tpu as pltpu
from jax.sharding import PartitionSpec as P

BINS = 1024
LAGS = 256
SRC = 16
STEPS = 4
WIN_DEV = 8
N_Z = 16
N_WIN = 8
N_STA = 64
LANES = 128
CHUNKS = BINS // LANES
GROUPS = BINS // SRC
WIDTH = BINS + LANES
PIECE_ROWS = 72

QUAD = [[32 * h + 2 * z + c for h in range(2) for c in range(2)] for z in range(N_Z)]
ALONG_Z = [[32 * h + 2 * z + c for z in range(N_Z)] for h in range(2) for c in range(2)]
ALL_QUADS = [
    [w * N_STA + 32 * h + 2 * z + c for w in range(N_WIN) for h in range(2) for c in range(2)]
    for z in range(N_Z)
]
MASKS = (0, 2, 1, 3)

SINE = (
    0.7071067690849304,
    -0.029462749138474464,
    0.0003682656097225845,
    -2.1877108338230755e-06,
    7.1552790359419305e-09,
)
COSINE = (
    1.4142135381698608,
    -0.17677636444568634,
    0.003682575421407819,
    -3.061264942516573e-05,
    1.2790856374067516e-07,
)


def xor_pairs(mask):
    return [(i, i ^ mask) for i in range(N_STA)]


def idft_table(bins, lags):
    frequency = jnp.arange(bins, dtype=jnp.int32)[None, :]
    lag_offset = jnp.arange(lags, dtype=jnp.int32)[:, None] - lags // 2
    phase_turns = jnp.mod(frequency * lag_offset, 2 * bins).astype(jnp.float32)
    angles = phase_turns * (math.pi / bins)
    return jnp.concatenate([jnp.cos(angles), -jnp.sin(angles)], 1).astype(jnp.bfloat16)


def cos_sin(x):
    square = x * x
    sine, cosine = SINE[-1], COSINE[-1]
    for a, b in zip(SINE[-2::-1], COSINE[-2::-1]):
        sine = sine * square + a
        cosine = cosine * square + b
    sine = sine * x
    return 1.0 - sine * sine, sine * cosine


def flag_column(flags, first):
    lanes = lax.broadcasted_iota(jnp.int32, flags.shape, 1)
    rows = lax.broadcasted_iota(jnp.int32, flags.shape, 0)
    return jnp.sum(jnp.where(lanes == rows + first, flags, 0.0), 1, keepdims=True)


def receivers_kernel(one_ref, two_ref, *out_refs):
    matrix_refs, flag_ref = out_refs[:CHUNKS], out_refs[CHUNKS]
    lanes = lax.broadcasted_iota(jnp.int32, (LANES, LANES), 1)
    for d in range(4):
        block = (one_ref, two_ref)[d // 2]
        marks = jnp.zeros((SRC, LANES), jnp.float32)
        for w in range(WIN_DEV):
            column = flag_column(block[d % 2, w, :, BINS:].astype(jnp.float32), SRC * w)
            marks = marks + jnp.where(lanes[:SRC] == w, column, 0.0)
        flag_ref[SRC * d : SRC * d + SRC, :] = marks.astype(jnp.bfloat16)

    def window(w, carry):
        columns = []
        for d in range(4):
            block = (one_ref, two_ref)[d // 2]
            columns.append(flag_column(block[d % 2, w, :, BINS:].astype(jnp.float32), SRC * w))
        for c in range(CHUNKS):
            real, imag = [], []
            for d in range(4):
                block = (one_ref, two_ref)[d // 2]
                phase = block[d % 2, w, :, LANES * c : LANES * c + LANES].astype(jnp.float32)
                re, im = cos_sin(phase)
                real.append(re * columns[d])
                imag.append(im * columns[d])
            over = jnp.concatenate(real + [-part for part in imag], 0).T
            rows = pl.ds(pl.multiple_of(SRC * w, SRC), SRC)
            for side, values in enumerate((over,)):
                cols = slice(LANES * side, LANES * side + LANES)
                values = values.astype(jnp.bfloat16)
                for k in range(LANES // SRC):
                    matrix_refs[c][k, rows, cols] = values[SRC * k : SRC * k + SRC]
        return carry

    lax.fori_loop(0, WIN_DEV, window, 0)


def receivers(one, two):
    return pl.pallas_call(
        receivers_kernel,
        out_shape=[jax.ShapeDtypeStruct((LANES // SRC, LANES, LANES), jnp.bfloat16)] * CHUNKS
        + [jax.ShapeDtypeStruct((4 * SRC, LANES), jnp.bfloat16)],
        compiler_params=pltpu.CompilerParams(vmem_limit_bytes=12 << 20),
        cost_estimate=pl.CostEstimate(
            flops=25 * 4 * SRC * WIN_DEV * BINS, bytes_accessed=10 << 20, transcendentals=0
        ),
        name="receivers",
    )(one, two)


def correlate_kernel(
    at_ref, src_ref, flag_ref, table_ref, *refs
):
    matrix_refs, (out_ref, spectra, order, by_group, stacked) = refs[:CHUNKS], refs[CHUNKS:]
    lanes = lax.broadcasted_iota(jnp.int32, (SRC, LANES), 1)
    rows = lax.broadcasted_iota(jnp.int32, (SRC, LANES), 0)
    place = at_ref[0]
    every = src_ref[:, BINS:].astype(jnp.float32)
    at = lax.broadcasted_iota(jnp.int32, every.shape, 0) == at_ref[1]
    column = flag_column(
        jnp.broadcast_to(jnp.sum(jnp.where(at, every, 0.0), 0, keepdims=True), every.shape), 0
    )
    marks = jnp.zeros((SRC, LANES), jnp.float32)
    for w in range(WIN_DEV):
        marks = marks + jnp.where(lanes == w, column[SRC * w : SRC * w + SRC], 0.0)
    marks = marks.astype(jnp.bfloat16)

    def prepare(c, carry):
        cols = pl.ds(pl.multiple_of(c * LANES, LANES), LANES)
        re, im = cos_sin(src_ref[:, cols].astype(jnp.float32))
        for part, values in enumerate((re * column, im * column)):
            to = pl.ds(pl.multiple_of(2 * SRC * c + SRC * part, SRC), SRC)
            for w in range(WIN_DEV):
                block = values[SRC * w : SRC * w + SRC].astype(jnp.bfloat16)
                spectra[to, LANES * w : LANES * w + LANES] = block
        return carry

    lax.fori_loop(0, CHUNKS, prepare, 0)
    square = (LANES, LANES)
    column = lax.broadcasted_iota(jnp.int32, square, 1)
    for k in range(LANES // SRC):
        taken = lax.broadcasted_iota(jnp.int32, square, 0) == SRC * k + lax.rem(column, SRC)
        for w in range(WIN_DEV):
            block = jnp.where(taken & (column // SRC == w), 1.0, 0.0).astype(jnp.bfloat16)
            first = LANES * (k % 2)
            order[k // 2, LANES * w : LANES * w + LANES, first : first + LANES] = block
    for k in range(0, LANES // SRC, 2):
        ordered = jnp.dot(spectra[...], order[k // 2], preferred_element_type=jnp.float32)
        by_group[k] = ordered[:, :LANES]
        by_group[k + 1] = ordered[:, LANES:]
    same_bin = lax.rem(lanes, SRC) == rows
    low = lanes < LANES // 2

    wide = lax.broadcasted_iota(jnp.int32, (LANES, LANES), 1) < LANES // 2
    minus_low = jnp.where(wide, -1.0, 1.0).astype(jnp.bfloat16)
    minus_high = jnp.where(wide, 1.0, -1.0).astype(jnp.bfloat16)
    for chunk in range(CHUNKS):
        for k in range(LANES // SRC):
            group = chunk * (LANES // SRC) + k
            left = []
            for s in range(SRC):
                parts = []
                for part in range(2):
                    row = by_group[k, pl.ds(2 * SRC * chunk + SRC * part + s, 1), :]
                    row = jnp.broadcast_to(row, (SRC, LANES))
                    parts.append(jnp.where(same_bin, row, 0.0).astype(jnp.bfloat16))
                left.append(jnp.concatenate(parts, 1))
            left = jnp.concatenate(left, 0)
            upper = matrix_refs[chunk][k]
            turned = jnp.concatenate([upper[:, LANES // 2 :], upper[:, : LANES // 2]], 1)
            lower = [turned * minus_low, upper * minus_high]
            right = [jnp.concatenate([upper, turned], 1), jnp.concatenate(lower, 1)]
            right = jnp.concatenate(right, 0)
            found = jnp.dot(left, right, preferred_element_type=jnp.float32)
            real = slice(SRC * group, SRC * group + SRC)
            imag = slice(BINS + SRC * group, BINS + SRC * group + SRC)
            for w in range(N_WIN):
                even = found[2 * SRC * w : 2 * SRC * w + SRC]
                odd = found[2 * SRC * w + SRC : 2 * SRC * w + 2 * SRC]
                cols = slice(LANES * w, LANES * w + LANES)
                stacked[real, cols] = jnp.where(low, even[:, :LANES], odd[:, LANES:]).astype(
                    jnp.bfloat16
                )
                stacked[imag, cols] = jnp.where(low, even[:, LANES:], odd[:, :LANES]).astype(
                    jnp.bfloat16
                )
    counts = []
    for d in range(4):
        count = lax.dot_general(
            marks,
            flag_ref[SRC * d : SRC * d + SRC, :],
            (((1,), (1,)), ((), ())),
            preferred_element_type=jnp.float32,
        )
        count = jnp.concatenate([count, jnp.zeros((SRC, LANES - SRC), jnp.float32)], 1)
        counts.append(count.astype(jnp.bfloat16))
    for pair in range(0, N_WIN, 2):
        cols = slice(LANES * pair, LANES * pair + 2 * LANES)
        lags = jnp.dot(table_ref[...], stacked[:, cols], preferred_element_type=jnp.float32)
        for w in range(pair, pair + 2):
            first = LANES * (w - pair)
            turned = lags[:, first : first + LANES].T.astype(jnp.bfloat16)
            for d in range(4):
                to = place ^ MASKS[d]
                for s in range(2):
                    part = turned[4 * SRC * s + SRC * d : 4 * SRC * s + SRC * d + SRC]
                    out_ref[w, to, SRC * s : SRC * s + SRC, :] = part[:, :LANES]
                    out_ref[w, to, 2 * SRC + SRC * s : 3 * SRC + SRC * s, :] = part[:, LANES:]
                up = 8 * (w // 4)
                out_ref[w, to, 64:PIECE_ROWS, :] = counts[d][up : up + 8]


def correlate(at, source, matrices, rec_flags, table):
    vmem = pl.BlockSpec(memory_space=pltpu.VMEM)
    return pl.pallas_call(
        correlate_kernel,
        out_shape=jax.ShapeDtypeStruct((N_WIN, 4, PIECE_ROWS, LANES), jnp.bfloat16),
        in_specs=[pl.BlockSpec(memory_space=pltpu.SMEM)] + [vmem] * (3 + CHUNKS),
        out_specs=vmem,
        scratch_shapes=[
            pltpu.VMEM((2 * SRC * CHUNKS, BINS), jnp.bfloat16),
            pltpu.VMEM((LANES // SRC // 2, BINS, 2 * LANES), jnp.bfloat16),
            pltpu.VMEM((LANES // SRC, 2 * SRC * CHUNKS, LANES), jnp.float32),
            pltpu.VMEM((2 * BINS, SRC * 4 * SRC), jnp.bfloat16),
        ],
        compiler_params=pltpu.CompilerParams(vmem_limit_bytes=20 << 20),
        cost_estimate=pl.CostEstimate(flops=1 << 30, bytes_accessed=12 << 20, transcendentals=0),
        name="correlate",
    )(at, source, rec_flags, table, *matrices)


def on_device(phases, validity, plan):
    me = lax.axis_index("sta")
    place = 2 * (me // 32) + lax.rem(me, 2)
    pieces = lax.all_to_all(
        phases.reshape(N_Z, 8, BINS), "sta", 0, 0, tiled=True, axis_index_groups=ALONG_Z
    )

    flags = validity.astype(jnp.bfloat16).reshape(1, 1, LANES)
    own = jnp.concatenate([phases, jnp.broadcast_to(flags, (WIN_DEV, SRC, LANES))], -1)
    across = lax.ppermute(own, "sta", xor_pairs(32))
    pieces, across = lax.optimization_barrier((pieces, across))
    one = jnp.stack([own, across], 0)
    two = lax.ppermute(one, "sta", xor_pairs(1))
    *matrices, rec_flags = receivers(one, two)

    owner_z = lax.rem(plan // 2, N_Z)
    held = jnp.stack(
        [lax.dynamic_index_in_dim(pieces, owner_z[k], 0, False) for k in range(STEPS)]
    )
    held = jnp.concatenate([held, jnp.broadcast_to(flags, (STEPS, 8, LANES))], -1)
    came = lax.all_to_all(held, "sta", 0, 0, tiled=True, axis_index_groups=QUAD)
    owner = plan[place]
    owner_place = 2 * (owner // 32) + lax.rem(owner, 2)
    mine = lax.dynamic_index_in_dim(came, owner_place, 0, False)[:, :BINS]
    quad_flags = came[:, :2, BINS:].reshape(8, LANES)
    sent = jnp.concatenate([mine, quad_flags], 1)
    source = lax.all_to_all(
        jnp.broadcast_to(sent[None], (N_Z, 8, WIDTH)),
        "sta",
        0,
        0,
        tiled=True,
        axis_index_groups=ALONG_Z,
    ).reshape(WIN_DEV * SRC, WIDTH)
    flag_row = 8 * lax.rem(owner // 2, N_Z) + 2 * owner_place

    sent = correlate(
        jnp.stack([place, flag_row]), source, matrices, rec_flags, idft_table(BINS, LAGS)
    )
    back = lax.all_to_all(
        sent.reshape(N_WIN * 4, PIECE_ROWS, LANES),
        ("win", "sta"),
        0,
        0,
        tiled=True,
        axis_index_groups=ALL_QUADS,
    )
    total = jnp.sum(back.reshape(N_WIN, 4, PIECE_ROWS, LANES).astype(jnp.float32), 0)
    lag_sum = total[:, :64].reshape(STEPS, 2, 2, SRC, LANES).transpose(0, 2, 3, 1, 4)
    lag_sum = lag_sum.reshape(STEPS, 2, SRC, LAGS)
    first = 64 + 2 * lax.rem(lax.axis_index("win"), 4)
    pair_count = lax.dynamic_slice(total, (0, first, 0), (STEPS, 2, SRC))
    factor = 1.0 / (math.sqrt(BINS) * jnp.sqrt(jnp.maximum(pair_count, 1.0)))
    return (lag_sum * factor[..., None]).astype(jnp.bfloat16)


def solution(mesh):
    return jax.shard_map(
        on_device,
        mesh=mesh,
        in_specs=(P("win", "sta", None), P("win", "sta"), P()),
        out_specs=P(None, "win", "sta", None),
        check_vma=False,
    )
```

time: 110 us -> 99.7 us (0.906)
  waiting for transfers between devices: 22.4 us -> 16.2 us
  Pallas kernels: 15 us -> 8.97 us
  starting transfers between devices: 51 us -> 52.8 us
    all_to_all x2, waiting for transfers between devices: 10.3 us -> 2.72 us  [the longest x1 2.72 us: on_device(): lax.all_to_all(jnp.broadcast_to(sent[None], (N_Z, 8, WIDTH)), 'sta', 0, 0...]
    pallas_call x1, Pallas kernels: 12.9 us -> 6.39 us  [correlate(): pl.pallas_call(correlate_kernel, out_shape=jax.ShapeDtypeStruct((N_WIN, 4...]
    all_to_all x1, starting transfers between devices: 10.9 us -> 12.9 us  [on_device(): lax.all_to_all(sent.reshape(N_WIN * 4, PIECE_ROWS, LANES), ('win', 'sta')...]
    all_to_all x1, starting transfers between devices: 10.8 us -> 9.05 us  [on_device(): came = lax.all_to_all(held, 'sta', 0, 0, tiled=True, axis_index_groups=QUAD)]
    all_to_all x1, waiting for transfers between devices: 0.01 us -> 1.35 us  [on_device(): came = lax.all_to_all(held, 'sta', 0, 0, tiled=True, axis_index_groups=QUAD)]
    all_to_all x2, starting transfers between devices: 21.7 us -> 23.1 us  [the longest x1 15.9 us: on_device(): lax.all_to_all(phases.reshape(N_Z, 8, BINS), 'sta', 0, 0, tiled=True, axi...]
  transfers between devices with their start and end apart: 6 -> 6, of which waited for: 3 -> 3; matrix products, arithmetic and copies ran while one was open for 6% -> 8% of each run, Pallas kernels for 2% -> 3%
where the time goes in v4:
time: 99.7 us; the launch traced here: 99 us
  starting transfers between devices  52.8 us (53%)
  waiting for transfers between devices  16.2 us (16%)
  between operations  10.4 us (10%)
  Pallas kernels  8.97 us (9%)
  other arithmetic  8.25 us (8%)
  local copies, waits for them, and re-layouts  2.39 us (2%)
    all_to_all x1, starting transfers between devices, on_device(): lax.all_to_all(phases.reshape(N_Z, 8, BINS), 'sta', 0, 0, tiled=True, axi...  15.9 us
    all_to_all x1, starting transfers between devices, on_device(): lax.all_to_all(sent.reshape(N_WIN * 4, PIECE_ROWS, LANES), ('win', 'sta')...  12.9 us
    all_to_all x1, waiting for transfers between devices, on_device(): lax.all_to_all(sent.reshape(N_WIN * 4, PIECE_ROWS, LANES), ('win', 'sta')...  12.2 us
    all_to_all x1, starting transfers between devices, on_device(): came = lax.all_to_all(held, 'sta', 0, 0, tiled=True, axis_index_groups=QUAD)  9.05 us
    all_to_all x1, starting transfers between devices, on_device(): lax.all_to_all(jnp.broadcast_to(sent[None], (N_Z, 8, WIDTH)), 'sta', 0, 0...  7.18 us
    pallas_call x1, Pallas kernels, correlate(): pl.pallas_call(correlate_kernel, out_shape=jax.ShapeDtypeStruct((N_WIN, 4...  6.39 us
    another operation x1, other arithmetic  4.84 us
    ppermute x1, starting transfers between devices, on_device(): across = lax.ppermute(own, 'sta', xor_pairs(32))  4.65 us
  transfers between devices with their start and end apart: 6, of which 3 were waited for; matrix products, arithmetic and copies ran while one was open for 8% of the time, Pallas kernels for 3%

profile of v4, /device:TPU:1, one launch (start us, length us, event | category | flops | bytes accessed | tf_op | source)
XLA Modules:
  0.0 99.0 jit_solution(11061556964117020011)
XLA Ops:
  0.0 0.0 copy-start
  0.0 15.9 %all-to-all-start = ((bf16[16,8,1024]{2,1,0:T(8,128)(2,1)}), bf16[16,8,1024]{2,1,0:T(8,128)(2,1)S(1)}, u32[]{:S(2)}, u32[]{:S(2)}) async-start(bf16[16,8,1024]{2,1,0:T(8,128)(2,1)} %bitcast.24), calls=%async_computation | async-start | bytes 524288 | tf_op jit(solution)/shard_map/all_to_all | solution.py:249
  15.9 0.7 convert_element_type.18
  16.6 0.1 reshape.38
  16.7 1.0 %fusion.7 = (bf16[1,8,16,1152]{3,2,1,0:T(8,128)(2,1)S(1)}, bf16[8,16,1152]{2,1,0:T(8,128)(2,1)S(1)}) fusion(bf16[1152]{0:T(1024)(128)(2,1)S(1)} %pad.12.clone, bf16[8,16,1024]{2,1,0:T(8,128)(2,1)} %param.3), kind=kLoop, calls=%fused_computation.34 | loop fusion | flops 589824 | bytes 854272 | tf_op jit(solution)/shard_map/stack | solution.py:257
  17.7 4.7 %collective-permute-start = (bf16[8,16,1152]{2,1,0:T(8,128)(2,1)S(1)}, bf16[8,16,1152]{2,1,0:T(8,128)(2,1)S(1)}, u32[]{:S(2)}, u32[]{:S(2)}) collective-permute-start(bf16[8,16,1152]{2,1,0:T(8,128)(2,1)S(1)} %get-tuple-element.28), channel_id=1, source_target_pairs={{0,256},{8,264},{16,272},{24,280},{32,288},{40,296},{48,304},{56,3... | collective-permute-start | bytes 884744 | tf_op jit(solution)/shard_map/ppermute | solution.py:255
  22.4 0.0 copy-done
  22.4 0.6 fusion.8
  30.4 0.0 collective-permute-done
  30.4 0.0 all-to-all-done
  30.4 0.6 maximum_maximum_fusion
  31.1 9.1 %all-to-all-start.1 = ((bf16[4,8,1152]{2,1,0:T(8,128)(2,1)}), bf16[4,8,1152]{2,1,0:T(8,128)(2,1)S(1)}, u32[]{:S(2)}, u32[]{:S(2)}) async-start(bf16[4,8,1152]{2,1,0:T(8,128)(2,1)} %maximum_maximum_fusion), calls=%async_computation.1 | async-start | bytes 147456 | tf_op jit(solution)/shard_map/all_to_all | solution.py:266
  40.1 0.7 dynamic_slice.23
  43.6 1.3 %all-to-all-done.1 = bf16[4,8,1152]{2,1,0:T(8,128)(2,1)S(1)} async-done(((bf16[4,8,1152]{2,1,0:T(8,128)(2,1)}), bf16[4,8,1152]{2,1,0:T(8,128)(2,1)S(1)}, u32[]{:S(2)}, u32[]{:S(2)}) %all-to-all-start.1) | async-done | bytes 73760 | tf_op jit(solution)/shard_map/all_to_all | solution.py:266
  45.0 0.7 broadcast_in_dim.11
  45.7 7.2 %all-to-all-start.2 = ((bf16[16,8,1152]{2,1,0:T(8,128)(2,1)}), bf16[16,8,1152]{2,1,0:T(8,128)(2,1)S(1)}, u32[]{:S(2)}, u32[]{:S(2)}) async-start(bf16[16,8,1152]{2,1,0:T(8,128)(2,1)} %broadcast_in_dim.11), calls=%async_computation.2 | async-start | bytes 589824 | tf_op jit(solution)/shard_map/all_to_all | solution.py:272
  52.9 0.1 pad_maximum_fusion.1.one_ref
  53.0 3.1 %collective-permute-start.1 = (bf16[2,8,16,1152]{3,2,1,0:T(8,128)(2,1)S(1)}, bf16[2,8,16,1152]{3,2,1,0:T(8,128)(2,1)S(1)}, u32[]{:S(2)}, u32[]{:S(2)}) collective-permute-start(bf16[2,8,16,1152]{3,2,1,0:T(8,128)(2,1)S(1)} %pad_maximum_fusion.1.one_ref), channel_id=1, source_target_pairs={{0,8},{8,0},{16,24},{24,16},{32,40},{40,32},{48,56},{56,48},{64,72... | collective-permute-start | bytes 1769480 | tf_op jit(solution)/shard_map/ppermute | solution.py:258
  56.1 0.1 pad_add_fusion.at_ref
  56.2 4.8 %cosine_convert_fusion = (bf16[256,1024]{1,0:T(8,128)(2,1)S(1)}, bf16[256,1024]{1,0:T(8,128)(2,1)S(1)}) fusion(s32[256]{0:T(256)S(1)} %iota_add_fusion), kind=kLoop, calls=%fused_computation.9 | loop fusion | flops 4456448 | bytes 1049600 | tf_op jit(solution)/shard_map/convert.1
  61.0 0.1 pad_maximum_fusion.table_ref
  61.1 0.0 collective-permute-done.1.two_ref
  61.1 2.6 %receivers.1 = (bf16[8,128,128]{2,1,0:T(8,128)(2,1)S(1)}, bf16[8,128,128]{2,1,0:T(8,128)(2,1)S(1)}, bf16[8,128,128]{2,1,0:T(8,128)(2,1)S(1)}, bf16[8,128,128]{2,...) custom-call(bf16[2,8,16,1152]{3,2,1,0:T(8,128)(2,1)S(1)} %pad_maximu, ...), custom_call_target="tpu_custom_call" | custom-call | flops 13107200 | bytes 10485760 | tf_op jit(solution)/shard_map/receivers/pallas_call | solution.py:113
  63.7 2.7 %all-to-all-done.2 = bf16[16,8,1152]{2,1,0:T(8,128)(2,1)S(1)} async-done(((bf16[16,8,1152]{2,1,0:T(8,128)(2,1)}), bf16[16,8,1152]{2,1,0:T(8,128)(2,1)S(1)}, u32[]{:S(2)}, u32[]{:S(2)}) %all-to-all-start.2) | async-done | bytes 294944 | tf_op jit(solution)/shard_map/all_to_all | solution.py:272
  66.4 6.4 %correlate.1 = bf16[8,4,72,128]{3,2,1,0:T(8,128)(2,1)} custom-call(s32[2]{0:T(128)S(1)} %pad_add_fusion.at_ref, bf16[128,1152]{1,0:T(8,128)(2,1)S(1)} %bitcast.22, bf16[64,128]{1,0:T(8,128)(2,1)S(1)} %get-tuple-element.18.flag_ref, bf16[256,2048]{1,0:T(8,128)(2,1)S(1)} %pad_maximum_fusion.table_ref, bf16[8,128,128]{2,1,0:T(8,128)(2,1)S(1)} %get-tuple-element.19.refs_0_, ...), custom_call_target="tpu_custom_call" | custom-call | flops 1073741824 | bytes 12582912 | tf_op jit(solution)/shard_map/correlate/pallas_call | solution.py:229
  72.8 12.9 %all-to-all-start.3 = ((bf16[32,72,128]{2,1,0:T(8,128)(2,1)}), bf16[32,72,128]{2,1,0:T(8,128)(2,1)S(1)}, u32[]{:S(2)}, u32[]{:S(2)}) async-start(bf16[32,72,128]{2,1,0:T(8,128)(2,1)} %bitcast.13), calls=%async_computation.3 | async-start | bytes 1179648 | tf_op jit(solution)/shard_map/all_to_all | solution.py:285
  85.7 12.2 %all-to-all-done.3 = bf16[32,72,128]{2,1,0:T(8,128)(2,1)S(1)} async-done(((bf16[32,72,128]{2,1,0:T(8,128)(2,1)}), bf16[32,72,128]{2,1,0:T(8,128)(2,1)S(1)}, u32[]{:S(2)}, u32[]{:S(2)}) %all-to-all-start.3) | async-done | bytes 589856 | tf_op jit(solution)/shard_map/all_to_all | solution.py:285
  97.9 0.1 convert_reduce_fusion
  98.0 0.1 copy.6
  98.1 0.1 reshape.35
  98.2 0.7 multiply_convert_fusion
  (10 shorter events, 0.1 us)
Async XLA Ops:
  0.0 22.4 %copy-start = (s32[4]{0:T(128)S(1)}, s32[4]{0:T(128)}, u32[]{:S(2)}) copy-start(s32[4]{0:T(128)} %param.5) | copy-start | bytes 52
  0.0 30.4 %all-to-all-start = ((bf16[16,8,1024]{2,1,0:T(8,128)(2,1)}), bf16[16,8,1024]{2,1,0:T(8,128)(2,1)S(1)}, u32[]{:S(2)}, u32[]{:S(2)}) async-start(bf16[16,8,1024]{2,1,0:T(8,128)(2,1)} %bitcast.24), calls=%async_computation | async-start | bytes 524288 | tf_op jit(solution)/shard_map/all_to_all | solution.py:249
  17.7 12.7 %collective-permute-start = (bf16[8,16,1152]{2,1,0:T(8,128)(2,1)S(1)}, bf16[8,16,1152]{2,1,0:T(8,128)(2,1)S(1)}, u32[]{:S(2)}, u32[]{:S(2)}) collective-permute-start(bf16[8,16,1152]{2,1,0:T(8,128)(2,1)S(1)} %get-tuple-element.28), channel_id=1, source_target_pairs={{0,256},{8,264},{16,272},{24,280},{32,288},{40,296},{48,304},{56,3... | collective-permute-start | bytes 884744 | tf_op jit(solution)/shard_map/ppermute | solution.py:255
  31.1 13.8 %all-to-all-start.1 = ((bf16[4,8,1152]{2,1,0:T(8,128)(2,1)}), bf16[4,8,1152]{2,1,0:T(8,128)(2,1)S(1)}, u32[]{:S(2)}, u32[]{:S(2)}) async-start(bf16[4,8,1152]{2,1,0:T(8,128)(2,1)} %maximum_maximum_fusion), calls=%async_computation.1 | async-start | bytes 147456 | tf_op jit(solution)/shard_map/all_to_all | solution.py:266
  45.7 20.7 %all-to-all-start.2 = ((bf16[16,8,1152]{2,1,0:T(8,128)(2,1)}), bf16[16,8,1152]{2,1,0:T(8,128)(2,1)S(1)}, u32[]{:S(2)}, u32[]{:S(2)}) async-start(bf16[16,8,1152]{2,1,0:T(8,128)(2,1)} %broadcast_in_dim.11), calls=%async_computation.2 | async-start | bytes 589824 | tf_op jit(solution)/shard_map/all_to_all | solution.py:272
  53.0 8.1 %collective-permute-start.1 = (bf16[2,8,16,1152]{3,2,1,0:T(8,128)(2,1)S(1)}, bf16[2,8,16,1152]{3,2,1,0:T(8,128)(2,1)S(1)}, u32[]{:S(2)}, u32[]{:S(2)}) collective-permute-start(bf16[2,8,16,1152]{3,2,1,0:T(8,128)(2,1)S(1)} %pad_maximum_fusion.1.one_ref), channel_id=1, source_target_pairs={{0,8},{8,0},{16,24},{24,16},{32,40},{40,32},{48,56},{56,48},{64,72... | collective-permute-start | bytes 1769480 | tf_op jit(solution)/shard_map/ppermute | solution.py:258
  72.8 25.1 %all-to-all-start.3 = ((bf16[32,72,128]{2,1,0:T(8,128)(2,1)}), bf16[32,72,128]{2,1,0:T(8,128)(2,1)S(1)}, u32[]{:S(2)}, u32[]{:S(2)}) async-start(bf16[32,72,128]{2,1,0:T(8,128)(2,1)} %bitcast.13), calls=%async_computation.3 | async-start | bytes 1179648 | tf_op jit(solution)/shard_map/all_to_all | solution.py:285

commit v5 on v4

--- a/solution.py
+++ b/solution.py
@@ -140,16 +140,17 @@
     marks = marks.astype(jnp.bfloat16)
 
     def prepare(c, carry):
-        cols = pl.ds(pl.multiple_of(c * LANES, LANES), LANES)
+        cols = slice(c * LANES, c * LANES + LANES)
         re, im = cos_sin(src_ref[:, cols].astype(jnp.float32))
         for part, values in enumerate((re * column, im * column)):
-            to = pl.ds(pl.multiple_of(2 * SRC * c + SRC * part, SRC), SRC)
+            to = slice(2 * SRC * c + SRC * part, 2 * SRC * c + SRC * part + SRC)
             for w in range(WIN_DEV):
                 block = values[SRC * w : SRC * w + SRC].astype(jnp.bfloat16)
                 spectra[to, LANES * w : LANES * w + LANES] = block
         return carry
 
-    lax.fori_loop(0, CHUNKS, prepare, 0)
+    for c in range(CHUNKS):
+        prepare(c, 0)
     square = (LANES, LANES)
     column = lax.broadcasted_iota(jnp.int32, square, 1)
     for k in range(LANES // SRC):
@@ -206,8 +207,7 @@
             (((1,), (1,)), ((), ())),
             preferred_element_type=jnp.float32,
         )
-        count = jnp.concatenate([count, jnp.zeros((SRC, LANES - SRC), jnp.float32)], 1)
-        counts.append(count.astype(jnp.bfloat16))
+        counts.append(jnp.concatenate([count, jnp.zeros((SRC, LANES - SRC), jnp.float32)], 1))
     for pair in range(0, N_WIN, 2):
         cols = slice(LANES * pair, LANES * pair + 2 * LANES)
         lags = jnp.dot(table_ref[...], stacked[:, cols], preferred_element_type=jnp.float32)
@@ -220,8 +220,9 @@
                     part = turned[4 * SRC * s + SRC * d : 4 * SRC * s + SRC * d + SRC]
                     out_ref[w, to, SRC * s : SRC * s + SRC, :] = part[:, :LANES]
                     out_ref[w, to, 2 * SRC + SRC * s : 3 * SRC + SRC * s, :] = part[:, LANES:]
-                up = 8 * (w // 4)
-                out_ref[w, to, 64:PIECE_ROWS, :] = counts[d][up : up + 8]
+                pair_counts = [counts[d][2 * w : 2 * w + 2], jnp.zeros((6, LANES), jnp.float32)]
+                pair_counts = jnp.concatenate(pair_counts, 0).astype(jnp.bfloat16)
+                out_ref[w, to, 64:PIECE_ROWS, :] = pair_counts
 
 
 def correlate(at, source, matrices, rec_flags, table):
@@ -293,8 +294,7 @@
     total = jnp.sum(back.reshape(N_WIN, 4, PIECE_ROWS, LANES).astype(jnp.float32), 0)
     lag_sum = total[:, :64].reshape(STEPS, 2, 2, SRC, LANES).transpose(0, 2, 3, 1, 4)
     lag_sum = lag_sum.reshape(STEPS, 2, SRC, LAGS)
-    first = 64 + 2 * lax.rem(lax.axis_index("win"), 4)
-    pair_count = lax.dynamic_slice(total, (0, first, 0), (STEPS, 2, SRC))
+    pair_count = total[:, 64:66, :SRC]
     factor = 1.0 / (math.sqrt(BINS) * jnp.sqrt(jnp.maximum(pair_count, 1.0)))
     return (lag_sum * factor[..., None]).astype(jnp.bfloat16)
 

time: 99.7 us -> 98 us (0.983)
  blocking collectives: 0 us -> 24.6 us
  starting transfers between devices: 52.8 us -> 39.8 us
  waiting for transfers between devices: 16.2 us -> 4.33 us
  Pallas kernels: 8.97 us -> 7.84 us
    all_to_all x0 -> x1, blocking collectives: none -> 24.6 us  [on_device(): lax.all_to_all(sent.reshape(N_WIN * 4, PIECE_ROWS, LANES), ('win', 'sta')...]
    all_to_all x1 -> x0, starting transfers between devices: 12.9 us -> none  [on_device(): lax.all_to_all(sent.reshape(N_WIN * 4, PIECE_ROWS, LANES), ('win', 'sta')...]
    all_to_all x1 -> x0, waiting for transfers between devices: 12.2 us -> none  [on_device(): lax.all_to_all(sent.reshape(N_WIN * 4, PIECE_ROWS, LANES), ('win', 'sta')...]
    pallas_call x1, Pallas kernels: 6.39 us -> 5.27 us  [correlate(): pl.pallas_call(correlate_kernel, out_shape=jax.ShapeDtypeStruct((N_WIN, 4...]
  transfers between devices with their start and end apart: 6 -> 5, of which waited for: 3 -> 2; matrix products, arithmetic and copies ran while one was open for 8% -> 8% of each run, Pallas kernels for 3% -> 3%
where the time goes in v5:
time: 98 us; the launch traced here: 97.4 us
  starting transfers between devices  39.8 us (41%)
  blocking collectives  24.6 us (25%)
  between operations  10.2 us (10%)
  other arithmetic  8.25 us (8%)
  Pallas kernels  7.84 us (8%)
  waiting for transfers between devices  4.33 us (4%)
  local copies, waits for them, and re-layouts  2.33 us (2%)
    all_to_all x1, blocking collectives, on_device(): lax.all_to_all(sent.reshape(N_WIN * 4, PIECE_ROWS, LANES), ('win', 'sta')...  24.6 us
    all_to_all x1, starting transfers between devices, on_device(): lax.all_to_all(phases.reshape(N_Z, 8, BINS), 'sta', 0, 0, tiled=True, axi...  15.9 us
    all_to_all x1, starting transfers between devices, on_device(): came = lax.all_to_all(held, 'sta', 0, 0, tiled=True, axis_index_groups=QUAD)  9.03 us
    all_to_all x1, starting transfers between devices, on_device(): lax.all_to_all(jnp.broadcast_to(sent[None], (N_Z, 8, WIDTH)), 'sta', 0, 0...  7.2 us
    pallas_call x1, Pallas kernels, correlate(): pl.pallas_call(correlate_kernel, out_shape=jax.ShapeDtypeStruct((N_WIN, 4...  5.27 us
    another operation x1, other arithmetic  4.84 us
    ppermute x1, starting transfers between devices, on_device(): across = lax.ppermute(own, 'sta', xor_pairs(32))  4.65 us
    ppermute x1, starting transfers between devices, on_device(): two = lax.ppermute(one, 'sta', xor_pairs(1))  3.08 us
  transfers between devices with their start and end apart: 5, of which 2 were waited for; matrix products, arithmetic and copies ran while one was open for 8% of the time, Pallas kernels for 3%

profile of v5, /device:TPU:1, one launch (start us, length us, event | category | flops | bytes accessed | tf_op | source)
XLA Modules:
  0.0 97.4 jit_solution(14658458478844337933)
XLA Ops:
  0.0 0.0 copy-start
  0.0 15.9 %all-to-all-start = ((bf16[16,8,1024]{2,1,0:T(8,128)(2,1)}), bf16[16,8,1024]{2,1,0:T(8,128)(2,1)S(1)}, u32[]{:S(2)}, u32[]{:S(2)}) async-start(bf16[16,8,1024]{2,1,0:T(8,128)(2,1)} %bitcast.25), calls=%async_computation | async-start | bytes 524288 | tf_op jit(solution)/shard_map/all_to_all | solution.py:250
  15.9 0.7 convert_element_type.18
  16.6 0.1 reshape.38
  16.7 1.0 %fusion.10 = (bf16[1,8,16,1152]{3,2,1,0:T(8,128)(2,1)S(1)}, bf16[8,16,1152]{2,1,0:T(8,128)(2,1)S(1)}) fusion(bf16[1152]{0:T(1024)(128)(2,1)S(1)} %pad.12.clone, bf16[8,16,1024]{2,1,0:T(8,128)(2,1)} %param.3), kind=kLoop, calls=%fused_computation.37 | loop fusion | flops 589824 | bytes 854272 | tf_op jit(solution)/shard_map/stack | solution.py:258
  17.7 4.7 %collective-permute-start = (bf16[8,16,1152]{2,1,0:T(8,128)(2,1)S(1)}, bf16[8,16,1152]{2,1,0:T(8,128)(2,1)S(1)}, u32[]{:S(2)}, u32[]{:S(2)}) collective-permute-start(bf16[8,16,1152]{2,1,0:T(8,128)(2,1)S(1)} %get-tuple-element.28), channel_id=1, source_target_pairs={{0,256},{8,264},{16,272},{24,280},{32,288},{40,296},{48,304},{56,3... | collective-permute-start | bytes 884744 | tf_op jit(solution)/shard_map/ppermute | solution.py:256
  22.4 0.0 copy-done
  22.4 0.6 fusion.11
  30.4 0.0 collective-permute-done
  30.4 0.0 all-to-all-done
  30.5 0.6 maximum_maximum_fusion
  31.1 9.0 %all-to-all-start.1 = ((bf16[4,8,1152]{2,1,0:T(8,128)(2,1)}), bf16[4,8,1152]{2,1,0:T(8,128)(2,1)S(1)}, u32[]{:S(2)}, u32[]{:S(2)}) async-start(bf16[4,8,1152]{2,1,0:T(8,128)(2,1)} %maximum_maximum_fusion), calls=%async_computation.1 | async-start | bytes 147456 | tf_op jit(solution)/shard_map/all_to_all | solution.py:267
  40.1 0.6 dynamic_slice.20
  43.3 1.6 %all-to-all-done.1 = bf16[4,8,1152]{2,1,0:T(8,128)(2,1)S(1)} async-done(((bf16[4,8,1152]{2,1,0:T(8,128)(2,1)}), bf16[4,8,1152]{2,1,0:T(8,128)(2,1)S(1)}, u32[]{:S(2)}, u32[]{:S(2)}) %all-to-all-start.1) | async-done | bytes 73760 | tf_op jit(solution)/shard_map/all_to_all | solution.py:267
  45.0 0.7 broadcast_in_dim.11
  45.7 7.2 %all-to-all-start.2 = ((bf16[16,8,1152]{2,1,0:T(8,128)(2,1)}), bf16[16,8,1152]{2,1,0:T(8,128)(2,1)S(1)}, u32[]{:S(2)}, u32[]{:S(2)}) async-start(bf16[16,8,1152]{2,1,0:T(8,128)(2,1)} %broadcast_in_dim.11), calls=%async_computation.2 | async-start | bytes 589824 | tf_op jit(solution)/shard_map/all_to_all | solution.py:273
  52.9 0.1 pad_maximum_fusion.1.one_ref
  53.0 3.1 %collective-permute-start.1 = (bf16[2,8,16,1152]{3,2,1,0:T(8,128)(2,1)S(1)}, bf16[2,8,16,1152]{3,2,1,0:T(8,128)(2,1)S(1)}, u32[]{:S(2)}, u32[]{:S(2)}) collective-permute-start(bf16[2,8,16,1152]{3,2,1,0:T(8,128)(2,1)S(1)} %pad_maximum_fusion.1.one_ref), channel_id=1, source_target_pairs={{0,8},{8,0},{16,24},{24,16},{32,40},{40,32},{48,56},{56,48},{64,72... | collective-permute-start | bytes 1769480 | tf_op jit(solution)/shard_map/ppermute | solution.py:259
  56.1 0.1 pad_add_fusion.at_ref
  56.2 4.8 %cosine_convert_fusion = (bf16[256,1024]{1,0:T(8,128)(2,1)S(1)}, bf16[256,1024]{1,0:T(8,128)(2,1)S(1)}) fusion(s32[256]{0:T(256)S(1)} %iota_add_fusion), kind=kLoop, calls=%fused_computation.9 | loop fusion | flops 4456448 | bytes 1049600 | tf_op jit(solution)/shard_map/convert.1
  61.0 0.1 pad_maximum_fusion.table_ref
  61.1 0.0 collective-permute-done.1.two_ref
  61.1 2.6 %receivers.1 = (bf16[8,128,128]{2,1,0:T(8,128)(2,1)S(1)}, bf16[8,128,128]{2,1,0:T(8,128)(2,1)S(1)}, bf16[8,128,128]{2,1,0:T(8,128)(2,1)S(1)}, bf16[8,128,128]{2,...) custom-call(bf16[2,8,16,1152]{3,2,1,0:T(8,128)(2,1)S(1)} %pad_maximu, ...), custom_call_target="tpu_custom_call" | custom-call | flops 13107200 | bytes 10485760 | tf_op jit(solution)/shard_map/receivers/pallas_call | solution.py:113
  63.7 2.7 %all-to-all-done.2 = bf16[16,8,1152]{2,1,0:T(8,128)(2,1)S(1)} async-done(((bf16[16,8,1152]{2,1,0:T(8,128)(2,1)}), bf16[16,8,1152]{2,1,0:T(8,128)(2,1)S(1)}, u32[]{:S(2)}, u32[]{:S(2)}) %all-to-all-start.2) | async-done | bytes 294944 | tf_op jit(solution)/shard_map/all_to_all | solution.py:273
  66.4 5.3 %correlate.1 = bf16[8,4,72,128]{3,2,1,0:T(8,128)(2,1)S(1)} custom-call(s32[2]{0:T(128)S(1)} %pad_add_fusion.at_ref, bf16[128,1152]{1,0:T(8,128)(2,1)S(1)} %bitcast.23, bf16[64,128]{1,0:T(8,128)(2,1)S(1)} %get-tuple-element.18.flag_ref, bf16[256,2048]{1,0:T(8,128)(2,1)S(1)} %pad_maximum_fusion.table_ref, bf16[8,128,128]{2,1,0:T(8,128)(2,1)S(1)} %get-tuple-element.19.refs_0_, ...), custom_call_target="tpu_custom_call" | custom-call | flops 1073741824 | bytes 12582912 | tf_op jit(solution)/shard_map/correlate/pallas_call | solution.py:230
  71.7 24.6 %all_to_all.20 = bf16[32,72,128]{2,1,0:T(8,128)(2,1)S(1)} all-to-all(bf16[32,72,128]{2,1,0:T(8,128)(2,1)S(1)} %bitcast.22), channel_id=1, replica_groups={{0,8,256,264,1,9,257,265,2,10,258,266,3,11,259,267,4,12,260,268,5,13,26..., dimensions={0} | all-to-all | bytes 1179648 | tf_op jit(solution)/shard_map/all_to_all | solution.py:286
  96.3 0.1 convert_reduce_fusion
  96.4 0.1 copy.6
  96.6 0.1 reshape.35
  96.7 0.7 multiply_convert_fusion
  (10 shorter events, 0.1 us)
Async XLA Ops:
  0.0 22.4 %copy-start = (s32[4]{0:T(128)S(1)}, s32[4]{0:T(128)}, u32[]{:S(2)}) copy-start(s32[4]{0:T(128)} %param.5) | copy-start | bytes 52
  0.0 30.4 %all-to-all-start = ((bf16[16,8,1024]{2,1,0:T(8,128)(2,1)}), bf16[16,8,1024]{2,1,0:T(8,128)(2,1)S(1)}, u32[]{:S(2)}, u32[]{:S(2)}) async-start(bf16[16,8,1024]{2,1,0:T(8,128)(2,1)} %bitcast.25), calls=%async_computation | async-start | bytes 524288 | tf_op jit(solution)/shard_map/all_to_all | solution.py:250
  17.7 12.7 %collective-permute-start = (bf16[8,16,1152]{2,1,0:T(8,128)(2,1)S(1)}, bf16[8,16,1152]{2,1,0:T(8,128)(2,1)S(1)}, u32[]{:S(2)}, u32[]{:S(2)}) collective-permute-start(bf16[8,16,1152]{2,1,0:T(8,128)(2,1)S(1)} %get-tuple-element.28), channel_id=1, source_target_pairs={{0,256},{8,264},{16,272},{24,280},{32,288},{40,296},{48,304},{56,3... | collective-permute-start | bytes 884744 | tf_op jit(solution)/shard_map/ppermute | solution.py:256
  31.1 13.8 %all-to-all-start.1 = ((bf16[4,8,1152]{2,1,0:T(8,128)(2,1)}), bf16[4,8,1152]{2,1,0:T(8,128)(2,1)S(1)}, u32[]{:S(2)}, u32[]{:S(2)}) async-start(bf16[4,8,1152]{2,1,0:T(8,128)(2,1)} %maximum_maximum_fusion), calls=%async_computation.1 | async-start | bytes 147456 | tf_op jit(solution)/shard_map/all_to_all | solution.py:267
  45.7 20.7 %all-to-all-start.2 = ((bf16[16,8,1152]{2,1,0:T(8,128)(2,1)}), bf16[16,8,1152]{2,1,0:T(8,128)(2,1)S(1)}, u32[]{:S(2)}, u32[]{:S(2)}) async-start(bf16[16,8,1152]{2,1,0:T(8,128)(2,1)} %broadcast_in_dim.11), calls=%async_computation.2 | async-start | bytes 589824 | tf_op jit(solution)/shard_map/all_to_all | solution.py:273
  53.0 8.1 %collective-permute-start.1 = (bf16[2,8,16,1152]{3,2,1,0:T(8,128)(2,1)S(1)}, bf16[2,8,16,1152]{3,2,1,0:T(8,128)(2,1)S(1)}, u32[]{:S(2)}, u32[]{:S(2)}) collective-permute-start(bf16[2,8,16,1152]{3,2,1,0:T(8,128)(2,1)S(1)} %pad_maximum_fusion.1.one_ref), channel_id=1, source_target_pairs={{0,8},{8,0},{16,24},{24,16},{32,40},{40,32},{48,56},{56,48},{64,72... | collective-permute-start | bytes 1769480 | tf_op jit(solution)/shard_map/ppermute | solution.py:259

commit v6 on v5

--- a/solution.py
+++ b/solution.py
@@ -125,7 +125,7 @@
 def correlate_kernel(
     at_ref, src_ref, flag_ref, table_ref, *refs
 ):
-    matrix_refs, (out_ref, spectra, order, by_group, stacked) = refs[:CHUNKS], refs[CHUNKS:]
+    matrix_refs, (out_ref, by_group, stacked) = refs[:CHUNKS], refs[CHUNKS:]
     lanes = lax.broadcasted_iota(jnp.int32, (SRC, LANES), 1)
     rows = lax.broadcasted_iota(jnp.int32, (SRC, LANES), 0)
     place = at_ref[0]
@@ -144,25 +144,18 @@
         re, im = cos_sin(src_ref[:, cols].astype(jnp.float32))
         for part, values in enumerate((re * column, im * column)):
             to = slice(2 * SRC * c + SRC * part, 2 * SRC * c + SRC * part + SRC)
-            for w in range(WIN_DEV):
-                block = values[SRC * w : SRC * w + SRC].astype(jnp.bfloat16)
-                spectra[to, LANES * w : LANES * w + LANES] = block
+            for k in range(LANES // SRC):
+                found = None
+                for w in range(WIN_DEV):
+                    block = values[SRC * w : SRC * w + SRC]
+                    shift = SRC * ((w - k) % WIN_DEV)
+                    block = pltpu.roll(block, shift, 1) if shift else block
+                    found = block if found is None else jnp.where(lanes // SRC == w, block, found)
+                by_group[k, to, :] = found
         return carry
 
     for c in range(CHUNKS):
         prepare(c, 0)
-    square = (LANES, LANES)
-    column = lax.broadcasted_iota(jnp.int32, square, 1)
-    for k in range(LANES // SRC):
-        taken = lax.broadcasted_iota(jnp.int32, square, 0) == SRC * k + lax.rem(column, SRC)
-        for w in range(WIN_DEV):
-            block = jnp.where(taken & (column // SRC == w), 1.0, 0.0).astype(jnp.bfloat16)
-            first = LANES * (k % 2)
-            order[k // 2, LANES * w : LANES * w + LANES, first : first + LANES] = block
-    for k in range(0, LANES // SRC, 2):
-        ordered = jnp.dot(spectra[...], order[k // 2], preferred_element_type=jnp.float32)
-        by_group[k] = ordered[:, :LANES]
-        by_group[k + 1] = ordered[:, LANES:]
     same_bin = lax.rem(lanes, SRC) == rows
     low = lanes < LANES // 2
 
@@ -233,8 +226,6 @@
         in_specs=[pl.BlockSpec(memory_space=pltpu.SMEM)] + [vmem] * (3 + CHUNKS),
         out_specs=vmem,
         scratch_shapes=[
-            pltpu.VMEM((2 * SRC * CHUNKS, BINS), jnp.bfloat16),
-            pltpu.VMEM((LANES // SRC // 2, BINS, 2 * LANES), jnp.bfloat16),
             pltpu.VMEM((LANES // SRC, 2 * SRC * CHUNKS, LANES), jnp.float32),
             pltpu.VMEM((2 * BINS, SRC * 4 * SRC), jnp.bfloat16),
         ],

time: 98 us -> 97.6 us (level)
  no operation moved by 1% of the time
where the time goes in v6:
time: 97.6 us; the launch traced here: 97 us
  starting transfers between devices  39.8 us (41%)
  blocking collectives  24.6 us (25%)
  between operations  10.2 us (10%)
  other arithmetic  8.25 us (8%)
  Pallas kernels  7.45 us (8%)
  waiting for transfers between devices  4.33 us (4%)
  local copies, waits for them, and re-layouts  2.33 us (2%)
    all_to_all x1, blocking collectives, on_device(): lax.all_to_all(sent.reshape(N_WIN * 4, PIECE_ROWS, LANES), ('win', 'sta')...  24.6 us
    all_to_all x1, starting transfers between devices, on_device(): lax.all_to_all(phases.reshape(N_Z, 8, BINS), 'sta', 0, 0, tiled=True, axi...  15.9 us
    all_to_all x1, starting transfers between devices, on_device(): came = lax.all_to_all(held, 'sta', 0, 0, tiled=True, axis_index_groups=QUAD)  9.03 us
    all_to_all x1, starting transfers between devices, on_device(): lax.all_to_all(jnp.broadcast_to(sent[None], (N_Z, 8, WIDTH)), 'sta', 0, 0...  7.2 us
    pallas_call x1, Pallas kernels, correlate(): pl.pallas_call(correlate_kernel, out_shape=jax.ShapeDtypeStruct((N_WIN, 4...  4.87 us
    another operation x1, other arithmetic  4.84 us
    ppermute x1, starting transfers between devices, on_device(): across = lax.ppermute(own, 'sta', xor_pairs(32))  4.65 us
    ppermute x1, starting transfers between devices, on_device(): two = lax.ppermute(one, 'sta', xor_pairs(1))  3.08 us
  transfers between devices with their start and end apart: 5, of which 2 were waited for; matrix products, arithmetic and copies ran while one was open for 8% of the time, Pallas kernels for 3%

profile of v6, /device:TPU:1, one launch (start us, length us, event | category | flops | bytes accessed | tf_op | source)
XLA Modules:
  0.0 97.0 jit_solution(14233615733784257656)
XLA Ops:
  0.0 0.0 copy-start
  0.0 15.9 %all-to-all-start = ((bf16[16,8,1024]{2,1,0:T(8,128)(2,1)}), bf16[16,8,1024]{2,1,0:T(8,128)(2,1)S(1)}, u32[]{:S(2)}, u32[]{:S(2)}) async-start(bf16[16,8,1024]{2,1,0:T(8,128)(2,1)} %bitcast.25), calls=%async_computation | async-start | bytes 524288 | tf_op jit(solution)/shard_map/all_to_all | solution.py:241
  15.9 0.7 convert_element_type.18
  16.6 0.1 reshape.38
  16.7 1.0 %fusion.10 = (bf16[1,8,16,1152]{3,2,1,0:T(8,128)(2,1)S(1)}, bf16[8,16,1152]{2,1,0:T(8,128)(2,1)S(1)}) fusion(bf16[1152]{0:T(1024)(128)(2,1)S(1)} %pad.12.clone, bf16[8,16,1024]{2,1,0:T(8,128)(2,1)} %param.3), kind=kLoop, calls=%fused_computation.37 | loop fusion | flops 589824 | bytes 854272 | tf_op jit(solution)/shard_map/stack | solution.py:249
  17.7 4.7 %collective-permute-start = (bf16[8,16,1152]{2,1,0:T(8,128)(2,1)S(1)}, bf16[8,16,1152]{2,1,0:T(8,128)(2,1)S(1)}, u32[]{:S(2)}, u32[]{:S(2)}) collective-permute-start(bf16[8,16,1152]{2,1,0:T(8,128)(2,1)S(1)} %get-tuple-element.28), channel_id=1, source_target_pairs={{0,256},{8,264},{16,272},{24,280},{32,288},{40,296},{48,304},{56,3... | collective-permute-start | bytes 884744 | tf_op jit(solution)/shard_map/ppermute | solution.py:247
  22.4 0.0 copy-done
  22.4 0.6 fusion.11
  30.4 0.0 collective-permute-done
  30.4 0.0 all-to-all-done
  30.5 0.6 maximum_maximum_fusion
  31.1 9.0 %all-to-all-start.1 = ((bf16[4,8,1152]{2,1,0:T(8,128)(2,1)}), bf16[4,8,1152]{2,1,0:T(8,128)(2,1)S(1)}, u32[]{:S(2)}, u32[]{:S(2)}) async-start(bf16[4,8,1152]{2,1,0:T(8,128)(2,1)} %maximum_maximum_fusion), calls=%async_computation.1 | async-start | bytes 147456 | tf_op jit(solution)/shard_map/all_to_all | solution.py:258
  40.1 0.6 dynamic_slice.20
  43.3 1.6 %all-to-all-done.1 = bf16[4,8,1152]{2,1,0:T(8,128)(2,1)S(1)} async-done(((bf16[4,8,1152]{2,1,0:T(8,128)(2,1)}), bf16[4,8,1152]{2,1,0:T(8,128)(2,1)S(1)}, u32[]{:S(2)}, u32[]{:S(2)}) %all-to-all-start.1) | async-done | bytes 73760 | tf_op jit(solution)/shard_map/all_to_all | solution.py:258
  45.0 0.7 broadcast_in_dim.11
  45.7 7.2 %all-to-all-start.2 = ((bf16[16,8,1152]{2,1,0:T(8,128)(2,1)}), bf16[16,8,1152]{2,1,0:T(8,128)(2,1)S(1)}, u32[]{:S(2)}, u32[]{:S(2)}) async-start(bf16[16,8,1152]{2,1,0:T(8,128)(2,1)} %broadcast_in_dim.11), calls=%async_computation.2 | async-start | bytes 589824 | tf_op jit(solution)/shard_map/all_to_all | solution.py:264
  52.9 0.1 pad_maximum_fusion.1.one_ref
  53.0 3.1 %collective-permute-start.1 = (bf16[2,8,16,1152]{3,2,1,0:T(8,128)(2,1)S(1)}, bf16[2,8,16,1152]{3,2,1,0:T(8,128)(2,1)S(1)}, u32[]{:S(2)}, u32[]{:S(2)}) collective-permute-start(bf16[2,8,16,1152]{3,2,1,0:T(8,128)(2,1)S(1)} %pad_maximum_fusion.1.one_ref), channel_id=1, source_target_pairs={{0,8},{8,0},{16,24},{24,16},{32,40},{40,32},{48,56},{56,48},{64,72... | collective-permute-start | bytes 1769480 | tf_op jit(solution)/shard_map/ppermute | solution.py:250
  56.1 0.1 pad_add_fusion.at_ref
  56.2 4.8 %cosine_convert_fusion = (bf16[256,1024]{1,0:T(8,128)(2,1)S(1)}, bf16[256,1024]{1,0:T(8,128)(2,1)S(1)}) fusion(s32[256]{0:T(256)S(1)} %iota_add_fusion), kind=kLoop, calls=%fused_computation.9 | loop fusion | flops 4456448 | bytes 1049600 | tf_op jit(solution)/shard_map/convert.1
  61.0 0.1 pad_maximum_fusion.table_ref
  61.1 0.0 collective-permute-done.1.two_ref
  61.1 2.6 %receivers.1 = (bf16[8,128,128]{2,1,0:T(8,128)(2,1)S(1)}, bf16[8,128,128]{2,1,0:T(8,128)(2,1)S(1)}, bf16[8,128,128]{2,1,0:T(8,128)(2,1)S(1)}, bf16[8,128,128]{2,...) custom-call(bf16[2,8,16,1152]{3,2,1,0:T(8,128)(2,1)S(1)} %pad_maximu, ...), custom_call_target="tpu_custom_call" | custom-call | flops 13107200 | bytes 10485760 | tf_op jit(solution)/shard_map/receivers/pallas_call | solution.py:113
  63.7 2.7 %all-to-all-done.2 = bf16[16,8,1152]{2,1,0:T(8,128)(2,1)S(1)} async-done(((bf16[16,8,1152]{2,1,0:T(8,128)(2,1)}), bf16[16,8,1152]{2,1,0:T(8,128)(2,1)S(1)}, u32[]{:S(2)}, u32[]{:S(2)}) %all-to-all-start.2) | async-done | bytes 294944 | tf_op jit(solution)/shard_map/all_to_all | solution.py:264
  66.4 4.9 %correlate.1 = bf16[8,4,72,128]{3,2,1,0:T(8,128)(2,1)S(1)} custom-call(s32[2]{0:T(128)S(1)} %pad_add_fusion.at_ref, bf16[128,1152]{1,0:T(8,128)(2,1)S(1)} %bitcast.23, bf16[64,128]{1,0:T(8,128)(2,1)S(1)} %get-tuple-element.18.flag_ref, bf16[256,2048]{1,0:T(8,128)(2,1)S(1)} %pad_maximum_fusion.table_ref, bf16[8,128,128]{2,1,0:T(8,128)(2,1)S(1)} %get-tuple-element.19.refs_0_, ...), custom_call_target="tpu_custom_call" | custom-call | flops 1073741824 | bytes 12582912 | tf_op jit(solution)/shard_map/correlate/pallas_call | solution.py:223
  71.3 24.6 %all_to_all.20 = bf16[32,72,128]{2,1,0:T(8,128)(2,1)S(1)} all-to-all(bf16[32,72,128]{2,1,0:T(8,128)(2,1)S(1)} %bitcast.22), channel_id=1, replica_groups={{0,8,256,264,1,9,257,265,2,10,258,266,3,11,259,267,4,12,260,268,5,13,26..., dimensions={0} | all-to-all | bytes 1179648 | tf_op jit(solution)/shard_map/all_to_all | solution.py:277
  95.9 0.1 convert_reduce_fusion
  96.0 0.1 copy.6
  96.2 0.1 reshape.35
  96.3 0.7 multiply_convert_fusion
  (10 shorter events, 0.1 us)
Async XLA Ops:
  0.0 22.4 %copy-start = (s32[4]{0:T(128)S(1)}, s32[4]{0:T(128)}, u32[]{:S(2)}) copy-start(s32[4]{0:T(128)} %param.5) | copy-start | bytes 52
  0.0 30.4 %all-to-all-start = ((bf16[16,8,1024]{2,1,0:T(8,128)(2,1)}), bf16[16,8,1024]{2,1,0:T(8,128)(2,1)S(1)}, u32[]{:S(2)}, u32[]{:S(2)}) async-start(bf16[16,8,1024]{2,1,0:T(8,128)(2,1)} %bitcast.25), calls=%async_computation | async-start | bytes 524288 | tf_op jit(solution)/shard_map/all_to_all | solution.py:241
  17.7 12.7 %collective-permute-start = (bf16[8,16,1152]{2,1,0:T(8,128)(2,1)S(1)}, bf16[8,16,1152]{2,1,0:T(8,128)(2,1)S(1)}, u32[]{:S(2)}, u32[]{:S(2)}) collective-permute-start(bf16[8,16,1152]{2,1,0:T(8,128)(2,1)S(1)} %get-tuple-element.28), channel_id=1, source_target_pairs={{0,256},{8,264},{16,272},{24,280},{32,288},{40,296},{48,304},{56,3... | collective-permute-start | bytes 884744 | tf_op jit(solution)/shard_map/ppermute | solution.py:247
  31.1 13.8 %all-to-all-start.1 = ((bf16[4,8,1152]{2,1,0:T(8,128)(2,1)}), bf16[4,8,1152]{2,1,0:T(8,128)(2,1)S(1)}, u32[]{:S(2)}, u32[]{:S(2)}) async-start(bf16[4,8,1152]{2,1,0:T(8,128)(2,1)} %maximum_maximum_fusion), calls=%async_computation.1 | async-start | bytes 147456 | tf_op jit(solution)/shard_map/all_to_all | solution.py:258
  45.7 20.7 %all-to-all-start.2 = ((bf16[16,8,1152]{2,1,0:T(8,128)(2,1)}), bf16[16,8,1152]{2,1,0:T(8,128)(2,1)S(1)}, u32[]{:S(2)}, u32[]{:S(2)}) async-start(bf16[16,8,1152]{2,1,0:T(8,128)(2,1)} %broadcast_in_dim.11), calls=%async_computation.2 | async-start | bytes 589824 | tf_op jit(solution)/shard_map/all_to_all | solution.py:264
  53.0 8.1 %collective-permute-start.1 = (bf16[2,8,16,1152]{3,2,1,0:T(8,128)(2,1)S(1)}, bf16[2,8,16,1152]{3,2,1,0:T(8,128)(2,1)S(1)}, u32[]{:S(2)}, u32[]{:S(2)}) collective-permute-start(bf16[2,8,16,1152]{3,2,1,0:T(8,128)(2,1)S(1)} %pad_maximum_fusion.1.one_ref), channel_id=1, source_target_pairs={{0,8},{8,0},{16,24},{24,16},{32,40},{40,32},{48,56},{56,48},{64,72... | collective-permute-start | bytes 1769480 | tf_op jit(solution)/shard_map/ppermute | solution.py:250

commit v7 on v6

--- a/solution.py
+++ b/solution.py
@@ -258,9 +258,7 @@
     came = lax.all_to_all(held, "sta", 0, 0, tiled=True, axis_index_groups=QUAD)
     owner = plan[place]
     owner_place = 2 * (owner // 32) + lax.rem(owner, 2)
-    mine = lax.dynamic_index_in_dim(came, owner_place, 0, False)[:, :BINS]
-    quad_flags = came[:, :2, BINS:].reshape(8, LANES)
-    sent = jnp.concatenate([mine, quad_flags], 1)
+    sent = lax.dynamic_index_in_dim(came, owner_place, 0, False)
     source = lax.all_to_all(
         jnp.broadcast_to(sent[None], (N_Z, 8, WIDTH)),
         "sta",
@@ -269,7 +267,7 @@
         tiled=True,
         axis_index_groups=ALONG_Z,
     ).reshape(WIN_DEV * SRC, WIDTH)
-    flag_row = 8 * lax.rem(owner // 2, N_Z) + 2 * owner_place
+    flag_row = 8 * lax.rem(owner // 2, N_Z)
 
     sent = correlate(
         jnp.stack([place, flag_row]), source, matrices, rec_flags, idft_table(BINS, LAGS)

time: 97.6 us -> 97.6 us (level)
  no operation moved by 1% of the time
where the time goes in v7:
time: 97.6 us; the launch traced here: 97 us
  starting transfers between devices  39.8 us (41%)
  blocking collectives  24.6 us (25%)
  between operations  10.2 us (10%)
  other arithmetic  8.24 us (8%)
  Pallas kernels  7.45 us (8%)
  waiting for transfers between devices  4.34 us (4%)
  local copies, waits for them, and re-layouts  2.32 us (2%)
    all_to_all x1, blocking collectives, on_device(): lax.all_to_all(sent.reshape(N_WIN * 4, PIECE_ROWS, LANES), ('win', 'sta')...  24.6 us
    all_to_all x1, starting transfers between devices, on_device(): lax.all_to_all(phases.reshape(N_Z, 8, BINS), 'sta', 0, 0, tiled=True, axi...  15.9 us
    all_to_all x1, starting transfers between devices, on_device(): came = lax.all_to_all(held, 'sta', 0, 0, tiled=True, axis_index_groups=QUAD)  9.03 us
    all_to_all x1, starting transfers between devices, on_device(): lax.all_to_all(jnp.broadcast_to(sent[None], (N_Z, 8, WIDTH)), 'sta', 0, 0...  7.2 us
    pallas_call x1, Pallas kernels, correlate(): pl.pallas_call(correlate_kernel, out_shape=jax.ShapeDtypeStruct((N_WIN, 4...  4.87 us
    another operation x1, other arithmetic  4.84 us
    ppermute x1, starting transfers between devices, on_device(): across = lax.ppermute(own, 'sta', xor_pairs(32))  4.65 us
    ppermute x1, starting transfers between devices, on_device(): two = lax.ppermute(one, 'sta', xor_pairs(1))  3.08 us
  transfers between devices with their start and end apart: 5, of which 2 were waited for; matrix products, arithmetic and copies ran while one was open for 8% of the time, Pallas kernels for 3%

profile of v7, /device:TPU:1, one launch (start us, length us, event | category | flops | bytes accessed | tf_op | source)
XLA Modules:
  0.0 97.0 jit_solution(16389375481795894038)
XLA Ops:
  0.0 0.0 copy-start
  0.0 15.9 %all-to-all-start = ((bf16[16,8,1024]{2,1,0:T(8,128)(2,1)}), bf16[16,8,1024]{2,1,0:T(8,128)(2,1)S(1)}, u32[]{:S(2)}, u32[]{:S(2)}) async-start(bf16[16,8,1024]{2,1,0:T(8,128)(2,1)} %bitcast.24), calls=%async_computation | async-start | bytes 524288 | tf_op jit(solution)/shard_map/all_to_all | solution.py:241
  15.9 0.7 convert_element_type.18
  16.6 0.1 reshape.33
  16.7 1.0 %fusion.10 = (bf16[1,8,16,1152]{3,2,1,0:T(8,128)(2,1)S(1)}, bf16[8,16,1152]{2,1,0:T(8,128)(2,1)S(1)}) fusion(bf16[1152]{0:T(1024)(128)(2,1)S(1)} %pad.10.clone, bf16[8,16,1024]{2,1,0:T(8,128)(2,1)} %param.3), kind=kLoop, calls=%fused_computation.36 | loop fusion | flops 589824 | bytes 854272 | tf_op jit(solution)/shard_map/stack | solution.py:249
  17.7 4.7 %collective-permute-start = (bf16[8,16,1152]{2,1,0:T(8,128)(2,1)S(1)}, bf16[8,16,1152]{2,1,0:T(8,128)(2,1)S(1)}, u32[]{:S(2)}, u32[]{:S(2)}) collective-permute-start(bf16[8,16,1152]{2,1,0:T(8,128)(2,1)S(1)} %get-tuple-element.28), channel_id=1, source_target_pairs={{0,256},{8,264},{16,272},{24,280},{32,288},{40,296},{48,304},{56,3... | collective-permute-start | bytes 884744 | tf_op jit(solution)/shard_map/ppermute | solution.py:247
  22.4 0.0 copy-done
  22.4 0.6 fusion.11
  30.4 0.0 collective-permute-done
  30.4 0.0 all-to-all-done
  30.5 0.6 maximum_maximum_fusion
  31.1 9.0 %all-to-all-start.1 = ((bf16[4,8,1152]{2,1,0:T(8,128)(2,1)}), bf16[4,8,1152]{2,1,0:T(8,128)(2,1)S(1)}, u32[]{:S(2)}, u32[]{:S(2)}) async-start(bf16[4,8,1152]{2,1,0:T(8,128)(2,1)} %maximum_maximum_fusion), calls=%async_computation.1 | async-start | bytes 147456 | tf_op jit(solution)/shard_map/all_to_all | solution.py:258
  40.1 0.6 dynamic_slice.20
  43.3 1.6 %all-to-all-done.1 = bf16[4,8,1152]{2,1,0:T(8,128)(2,1)S(1)} async-done(((bf16[4,8,1152]{2,1,0:T(8,128)(2,1)}), bf16[4,8,1152]{2,1,0:T(8,128)(2,1)S(1)}, u32[]{:S(2)}, u32[]{:S(2)}) %all-to-all-start.1) | async-done | bytes 73760 | tf_op jit(solution)/shard_map/all_to_all | solution.py:258
  44.9 0.7 broadcast_in_dim.27
  45.7 7.2 %all-to-all-start.2 = ((bf16[16,8,1152]{2,1,0:T(8,128)(2,1)}), bf16[16,8,1152]{2,1,0:T(8,128)(2,1)S(1)}, u32[]{:S(2)}, u32[]{:S(2)}) async-start(bf16[16,8,1152]{2,1,0:T(8,128)(2,1)} %broadcast_in_dim.27), calls=%async_computation.2 | async-start | bytes 589824 | tf_op jit(solution)/shard_map/all_to_all | solution.py:262
  52.9 0.1 pad_maximum_fusion.1.one_ref
  53.0 3.1 %collective-permute-start.1 = (bf16[2,8,16,1152]{3,2,1,0:T(8,128)(2,1)S(1)}, bf16[2,8,16,1152]{3,2,1,0:T(8,128)(2,1)S(1)}, u32[]{:S(2)}, u32[]{:S(2)}) collective-permute-start(bf16[2,8,16,1152]{3,2,1,0:T(8,128)(2,1)S(1)} %pad_maximum_fusion.1.one_ref), channel_id=1, source_target_pairs={{0,8},{8,0},{16,24},{24,16},{32,40},{40,32},{48,56},{56,48},{64,72... | collective-permute-start | bytes 1769480 | tf_op jit(solution)/shard_map/ppermute | solution.py:250
  56.1 0.1 pad_add_fusion.at_ref
  56.1 4.8 %cosine_convert_fusion = (bf16[256,1024]{1,0:T(8,128)(2,1)S(1)}, bf16[256,1024]{1,0:T(8,128)(2,1)S(1)}) fusion(s32[256]{0:T(256)S(1)} %iota_add_fusion), kind=kLoop, calls=%fused_computation.9 | loop fusion | flops 4456448 | bytes 1049600 | tf_op jit(solution)/shard_map/convert.1
  61.0 0.1 pad_maximum_fusion.table_ref
  61.1 0.0 collective-permute-done.1.two_ref
  61.1 2.6 %receivers.1 = (bf16[8,128,128]{2,1,0:T(8,128)(2,1)S(1)}, bf16[8,128,128]{2,1,0:T(8,128)(2,1)S(1)}, bf16[8,128,128]{2,1,0:T(8,128)(2,1)S(1)}, bf16[8,128,128]{2,...) custom-call(bf16[2,8,16,1152]{3,2,1,0:T(8,128)(2,1)S(1)} %pad_maximu, ...), custom_call_target="tpu_custom_call" | custom-call | flops 13107200 | bytes 10485760 | tf_op jit(solution)/shard_map/receivers/pallas_call | solution.py:113
  63.7 2.7 %all-to-all-done.2 = bf16[16,8,1152]{2,1,0:T(8,128)(2,1)S(1)} async-done(((bf16[16,8,1152]{2,1,0:T(8,128)(2,1)}), bf16[16,8,1152]{2,1,0:T(8,128)(2,1)S(1)}, u32[]{:S(2)}, u32[]{:S(2)}) %all-to-all-start.2) | async-done | bytes 294944 | tf_op jit(solution)/shard_map/all_to_all | solution.py:262
  66.4 4.9 %correlate.1 = bf16[8,4,72,128]{3,2,1,0:T(8,128)(2,1)S(1)} custom-call(s32[2]{0:T(128)S(1)} %pad_add_fusion.at_ref, bf16[128,1152]{1,0:T(8,128)(2,1)S(1)} %bitcast.22, bf16[64,128]{1,0:T(8,128)(2,1)S(1)} %get-tuple-element.18.flag_ref, bf16[256,2048]{1,0:T(8,128)(2,1)S(1)} %pad_maximum_fusion.table_ref, bf16[8,128,128]{2,1,0:T(8,128)(2,1)S(1)} %get-tuple-element.19.refs_0_, ...), custom_call_target="tpu_custom_call" | custom-call | flops 1073741824 | bytes 12582912 | tf_op jit(solution)/shard_map/correlate/pallas_call | solution.py:223
  71.3 24.6 %all_to_all.20 = bf16[32,72,128]{2,1,0:T(8,128)(2,1)S(1)} all-to-all(bf16[32,72,128]{2,1,0:T(8,128)(2,1)S(1)} %bitcast.21), channel_id=1, replica_groups={{0,8,256,264,1,9,257,265,2,10,258,266,3,11,259,267,4,12,260,268,5,13,26..., dimensions={0} | all-to-all | bytes 1179648 | tf_op jit(solution)/shard_map/all_to_all | solution.py:275
  95.9 0.1 convert_reduce_fusion
  96.0 0.1 copy.6
  96.1 0.1 reshape.30
  96.2 0.7 multiply_convert_fusion
  (7 shorter events, 0.1 us)
Async XLA Ops:
  0.0 22.4 %copy-start = (s32[4]{0:T(128)S(1)}, s32[4]{0:T(128)}, u32[]{:S(2)}) copy-start(s32[4]{0:T(128)} %param.5) | copy-start | bytes 52
  0.0 30.4 %all-to-all-start = ((bf16[16,8,1024]{2,1,0:T(8,128)(2,1)}), bf16[16,8,1024]{2,1,0:T(8,128)(2,1)S(1)}, u32[]{:S(2)}, u32[]{:S(2)}) async-start(bf16[16,8,1024]{2,1,0:T(8,128)(2,1)} %bitcast.24), calls=%async_computation | async-start | bytes 524288 | tf_op jit(solution)/shard_map/all_to_all | solution.py:241
  17.7 12.7 %collective-permute-start = (bf16[8,16,1152]{2,1,0:T(8,128)(2,1)S(1)}, bf16[8,16,1152]{2,1,0:T(8,128)(2,1)S(1)}, u32[]{:S(2)}, u32[]{:S(2)}) collective-permute-start(bf16[8,16,1152]{2,1,0:T(8,128)(2,1)S(1)} %get-tuple-element.28), channel_id=1, source_target_pairs={{0,256},{8,264},{16,272},{24,280},{32,288},{40,296},{48,304},{56,3... | collective-permute-start | bytes 884744 | tf_op jit(solution)/shard_map/ppermute | solution.py:247
  31.1 13.8 %all-to-all-start.1 = ((bf16[4,8,1152]{2,1,0:T(8,128)(2,1)}), bf16[4,8,1152]{2,1,0:T(8,128)(2,1)S(1)}, u32[]{:S(2)}, u32[]{:S(2)}) async-start(bf16[4,8,1152]{2,1,0:T(8,128)(2,1)} %maximum_maximum_fusion), calls=%async_computation.1 | async-start | bytes 147456 | tf_op jit(solution)/shard_map/all_to_all | solution.py:258
  45.7 20.7 %all-to-all-start.2 = ((bf16[16,8,1152]{2,1,0:T(8,128)(2,1)}), bf16[16,8,1152]{2,1,0:T(8,128)(2,1)S(1)}, u32[]{:S(2)}, u32[]{:S(2)}) async-start(bf16[16,8,1152]{2,1,0:T(8,128)(2,1)} %broadcast_in_dim.27), calls=%async_computation.2 | async-start | bytes 589824 | tf_op jit(solution)/shard_map/all_to_all | solution.py:262
  53.0 8.1 %collective-permute-start.1 = (bf16[2,8,16,1152]{3,2,1,0:T(8,128)(2,1)S(1)}, bf16[2,8,16,1152]{3,2,1,0:T(8,128)(2,1)S(1)}, u32[]{:S(2)}, u32[]{:S(2)}) collective-permute-start(bf16[2,8,16,1152]{3,2,1,0:T(8,128)(2,1)S(1)} %pad_maximum_fusion.1.one_ref), channel_id=1, source_target_pairs={{0,8},{8,0},{16,24},{24,16},{32,40},{40,32},{48,56},{56,48},{64,72... | collective-permute-start | bytes 1769480 | tf_op jit(solution)/shard_map/ppermute | solution.py:250
